TPU v7x, 32 devices: a whole 2x2x4 slice. The times are simulated.
32 devices in a mesh: ctx: 16 (over z, y, core), fsdp: 2 (over x).
Axes of the slice: x: 2, y: 2, z: 4, core: 2. Of those that a mesh axis runs over, the one named last changes fastest.
Arguments:
- inputs: bfloat16 [4, 8192, 1024], P('fsdp', 'ctx'), may hold values from -6 to 6
- cotangent: bfloat16 [4, 8192, 1024], P('fsdp', 'ctx'), may hold values from -6 to 6
- segments: int32 [4, 8192], P('fsdp'), may hold values from 0 to 7, as said below
- w_qkv: bfloat16 [1024, 3072], P('fsdp'), may hold values from -0.25 to 0.25
- w_out: bfloat16 [1024, 1024], P('fsdp'), may hold values from -0.75 to 0.75
- w_in: bfloat16 [1024, 5248], P('fsdp'), may hold values from -0.1875 to 0.1875
- w_down: bfloat16 [2624, 1024], P('fsdp'), may hold values from -0.125 to 0.125
- norm_gains: bfloat16 [2, 1024], P(None, 'fsdp'), may hold values from 0.5 to 1.5
- slot_table: int32 [2992], replicated, may hold values from 0 to 3007, as said below
- master: float32 [3008, 64, 64], P(('ctx', 'fsdp')), may hold values from -0.1875 to 0.1875
- first_moment: float32 [3008, 64, 64], P(('ctx', 'fsdp'))
- rotated_second_moments: float32 [3008, 64, 64], P(('ctx', 'fsdp')), may hold values from 16384 to 65536
- row_eigenbasis: float32 [3008, 64, 64], P(('ctx', 'fsdp')), may hold values from -0.75 to 0.75
- column_eigenbasis: float32 [3008, 64, 64], P(('ctx', 'fsdp')), may hold values from -0.75 to 0.75
- gain_master: float32 [2, 1024], replicated, may hold values from 0.5 to 1.5
- gain_first: float32 [2, 1024], replicated
- gain_second: float32 [2, 1024], replicated, may hold values from 16384 to 65536
Outputs:
- layer_out: bfloat16 [4, 8192, 1024], P('fsdp', 'ctx')
- input_grad: bfloat16 [4, 8192, 1024], P('fsdp', 'ctx')
- block_grads: float32 [3008, 64, 64], P(('ctx', 'fsdp'))
- gain_grads: float32 [2, 1024], replicated
- new_master: float32 [3008, 64, 64], P(('ctx', 'fsdp'))
- new_copy: bfloat16 [3008, 64, 64], P(('ctx', 'fsdp'))
- new_first: float32 [3008, 64, 64], P(('ctx', 'fsdp'))
- new_second: float32 [3008, 64, 64], P(('ctx', 'fsdp'))
- new_gains: float32 [2, 1024], replicated
- new_gain_first: float32 [2, 1024], replicated
- new_gain_second: float32 [2, 1024], replicated
Inputs may be any that keep to these rules, and one draw needn't show every extreme that they name: `segments`: document numbers never fall along a sequence; each sequence holds 8 documents of one or more positions each, exactly one of them 8192 // 2 positions long. `slot_table`: distinct slots; device r of ctx+fsdp (ctx the slower) holds slots r * 94 to r * 94 + 93; slots 0 and 3007 are in use.
All inputs are finite; a program needn't handle non-finite values.
Results may differ from a plain program's by a relative error of at most 0.02.
Values may be sent and summed in bfloat16 or wider, within the bound.
No kernel may reach another device: no remote copies, remote signals or barrier semaphores. Data moves between devices by JAX's collectives and lax.ppermute only.
A program may use at most 448 MiB of HBM per device.

v0:
```python
import functools
import jax, jax.numpy as jnp
from jax import lax
from jax.experimental import pallas as pl
from jax.experimental.pallas import tpu as pltpu
from jax.sharding import PartitionSpec as P

HEAD = 64
NDOC=8
BIG=1e30
LN2=0.6931471805599453
LOG2E=1.4426950408889634

def split3(v):
    hi=v.astype(jnp.bfloat16)
    r=v-hi.astype(jnp.float32)
    mid=r.astype(jnp.bfloat16)
    lo=(r-mid.astype(jnp.float32)).astype(jnp.bfloat16)
    return hi.astype(jnp.float32),mid.astype(jnp.float32),lo.astype(jnp.float32)

def doc_rows(seg_row):
    n=seg_row.shape[1]
    ids=lax.broadcasted_iota(jnp.int32,(NDOC,n),0)
    return (ids==seg_row).astype(jnp.float32)

def fwd_kernel(bq,bk,sub,lo_ref,hi_ref,qkv_ref,seg_ref,out_ref,raw_ref,lse_ref,q_s,k_s,v_s):
    chunks,_,width=qkv_ref.shape
    full=chunks*width
    def prep(c,carry):
        cols=pl.ds(pl.multiple_of(c*width,width),width)
        hot=doc_rows(seg_ref[:,cols])
        zero8=jnp.zeros((8,width),jnp.float32)
        q_s[0:64,cols]=qkv_ref[c,0:64,:]
        q_s[64:80,cols]=jnp.concatenate([hot,zero8],0).astype(jnp.bfloat16)
        kt=jnp.concatenate([qkv_ref[c,64:128,:].astype(jnp.float32),(hot-1.0)*BIG,jnp.zeros((56,width),jnp.float32)],0)
        k_s[cols,:]=kt.T.astype(jnp.bfloat16)
        v_s[0:64,cols]=qkv_ref[c,128:192,:]
        row=lax.broadcasted_iota(jnp.int32,(16,width),0)
        v_s[64:80,cols]=(row==0).astype(jnp.bfloat16)
        return carry
    lax.fori_loop(0,chunks,prep,0)
    def q_step(i,carry):
        cols=pl.ds(pl.multiple_of(i*bq,bq),bq)
        qa=q_s[:,cols]
        def k_step(j,state):
            rows=pl.ds(pl.multiple_of(j*bk,bk),bk)
            ka=k_s[rows,0:80]
            va=v_s[:,rows]
            new=[]
            for n in range(bq//sub):
                m,acc=state[n]
                s=jnp.dot(ka,qa[:,n*sub:(n+1)*sub],preferred_element_type=jnp.float32)
                m_new=jnp.maximum(m,jnp.max(s,axis=0,keepdims=True))
                p=jnp.exp2(s-m_new).astype(jnp.bfloat16)
                acc=acc*jnp.exp2(m-m_new)+jnp.dot(va,p,preferred_element_type=jnp.float32)
                new.append((m_new,acc))
            return tuple(new)
        init=tuple((jnp.full((1,sub),-3e38,jnp.float32),jnp.zeros((80,sub),jnp.float32)) for _ in range(bq//sub))
        state=lax.fori_loop(lo_ref[i],hi_ref[i],k_step,init)
        m=jnp.concatenate([s[0] for s in state],1); acc=jnp.concatenate([s[1] for s in state],1)
        total=acc[64:65]
        o=acc[0:64]/total
        raw_ref[:,cols]=o
        lse_ref[:,cols]=m+jnp.log2(total)
        return carry
    lax.fori_loop(0,full//bq,q_step,0)
    def emit(c,carry):
        cols=pl.ds(pl.multiple_of(c*width,width),width)
        out_ref[c]=raw_ref[:,cols].astype(jnp.bfloat16)
        return carry
    lax.fori_loop(0,chunks,emit,0)

def bwd_kernel(bq,bk,sub,lo_ref,hi_ref,qkv_ref,seg_ref,do_ref,raw_ref,lse_ref,cos_ref,sin_ref,out_ref,flat_ref,
               q_s,kt_s,k_s,vt_s,do_s,qdt_s,dkv_s):
    chunks,_,width=qkv_ref.shape
    full=chunks*width
    def prep(c,carry):
        cols=pl.ds(pl.multiple_of(c*width,width),width)
        hot=doc_rows(seg_ref[:,cols])
        row=lax.broadcasted_iota(jnp.int32,(8,width),0)
        ones3=(row<3).astype(jnp.float32)
        def three(v):
            a,b,d=split3(-v)
            return jnp.where(row==0,a,jnp.where(row==1,b,jnp.where(row==2,d,0.0)))
        qt=qkv_ref[c,0:64,:]
        kt=qkv_ref[c,64:128,:]
        dt=do_ref[c]
        kt_s[0:64,cols]=kt
        kt_s[64:80,cols]=jnp.concatenate([(hot-1.0)*BIG,ones3],0).astype(jnp.bfloat16)
        vt_s[0:64,cols]=qkv_ref[c,128:192,:]
        vt_s[64:80,cols]=jnp.concatenate([ones3,jnp.zeros((8,width),jnp.float32)],0).astype(jnp.bfloat16)
        qdt_s[0:64,cols]=qt
        qdt_s[64:128,cols]=dt
        qq=jnp.concatenate([qt.astype(jnp.float32),hot,three(lse_ref[:,cols]),jnp.zeros((48,width),jnp.float32)],0)
        q_s[cols,:]=qq.T.astype(jnp.bfloat16)
        df=dt.astype(jnp.float32)
        delta=jnp.sum(df*raw_ref[:,cols],axis=0,keepdims=True)
        dd=jnp.concatenate([df,three(delta),jnp.zeros((56,width),jnp.float32)],0)
        do_s[cols,:]=dd.T.astype(jnp.bfloat16)
        kk=jnp.concatenate([kt.astype(jnp.float32),jnp.zeros((64,width),jnp.float32)],0)
        k_s[cols,:]=kk.T.astype(jnp.bfloat16)
        dkv_s[:,cols]=jnp.zeros((128,width),jnp.float32)
        return carry
    lax.fori_loop(0,chunks,prep,0)
    def q_step(i,carry):
        cols=pl.ds(pl.multiple_of(i*bq,bq),bq)
        qt=qdt_s[0:64,cols]; dt=qdt_s[64:128,cols]
        def k_step(j,dq):
            keys=pl.ds(pl.multiple_of(j*bk,bk),bk)
            dqs=[]; ps=[]; dss=[]
            for r in range(bq//sub):
                rr=pl.ds(pl.multiple_of(i*bq+r*sub,sub),sub)
                s=jnp.dot(q_s[rr,0:80],kt_s[:,keys],preferred_element_type=jnp.float32)
                dp=jnp.dot(do_s[rr,0:80],vt_s[:,keys],preferred_element_type=jnp.float32)
                p=jnp.exp2(s)
                ps.append(p.astype(jnp.bfloat16))
                ds=(p*dp).astype(jnp.bfloat16)
                dss.append(ds)
                dqs.append(jnp.dot(ds,k_s[keys,:],preferred_element_type=jnp.float32))
            ds=jnp.concatenate(dss,0); p16=jnp.concatenate(ps,0)
            dkv_s[0:64,keys]+=jnp.dot(qt,ds,preferred_element_type=jnp.float32)
            dkv_s[64:128,keys]+=jnp.dot(dt,p16,preferred_element_type=jnp.float32)
            return dq+jnp.concatenate(dqs,0)
        dq=lax.fori_loop(lo_ref[i],hi_ref[i],k_step,jnp.zeros((bq,128),jnp.float32))
        dq=(dq*0.125).T[0:64]
        c=cos_ref[:,cols]; s=sin_ref[:,cols]
        a,b=dq[0:32],dq[32:64]
        rot=jnp.concatenate([a*c+b*s,b*c-a*s],0).astype(jnp.bfloat16)
        flat_ref[0:64,cols]=rot
        return carry
    lax.fori_loop(0,full//bq,q_step,0)
    def emit(c,carry):
        cols=pl.ds(pl.multiple_of(c*width,width),width)
        t=dkv_s[:,cols]
        dk=t[0:64]*LN2
        co=cos_ref[:,cols]; si=sin_ref[:,cols]
        a,b=dk[0:32],dk[32:64]
        v=jnp.concatenate([a*co+b*si,b*co-a*si,t[64:128]],0).astype(jnp.bfloat16)
        flat_ref[64:192,cols]=v
        out_ref[c,0:64,:]=flat_ref[0:64,cols]
        out_ref[c,64:192,:]=v
        return carry
    lax.fori_loop(0,chunks,emit,0)

def ranges(seg_row,bq,bk):
    full=seg_row.shape[0]
    firsts=seg_row[::bq]; lasts=seg_row[bq-1::bq]
    lo=jnp.sum((seg_row[None,:]<firsts[:,None]).astype(jnp.int32),axis=1)//bk
    hi=-(-jnp.sum((seg_row[None,:]<=lasts[:,None]).astype(jnp.int32),axis=1)//bk)
    return lo.astype(jnp.int32),hi.astype(jnp.int32)

VM=pl.BlockSpec(memory_space=pltpu.VMEM)
SM=pl.BlockSpec(memory_space=pltpu.SMEM)
def attend_forward(qkv,seg_row,bq=512,bk=512,sub=256):
    chunks,_,width=qkv.shape; full=chunks*width
    lo,hi=ranges(seg_row,bq,bk)
    return pl.pallas_call(functools.partial(fwd_kernel,bq,bk,sub),
      out_shape=(jax.ShapeDtypeStruct((chunks,64,width),jnp.bfloat16),jax.ShapeDtypeStruct((64,full),jnp.float32),jax.ShapeDtypeStruct((1,full),jnp.float32)),
      in_specs=[SM,SM,VM,VM],out_specs=(VM,VM,VM),
      scratch_shapes=[pltpu.VMEM((80,full),jnp.bfloat16),pltpu.VMEM((full,128),jnp.bfloat16),pltpu.VMEM((80,full),jnp.bfloat16)],
      compiler_params=pltpu.CompilerParams(vmem_limit_bytes=40<<20),
      cost_estimate=pl.CostEstimate(flops=1140*full*full,bytes_accessed=8<<20,transcendentals=0),
      name="attend_fwd")(lo,hi,qkv,seg_row[None,:])
def attend_backward(qkv,seg_row,do,raw,lse,cos,sin,bq=512,bk=512,sub=512):
    chunks,_,width=qkv.shape; full=chunks*width
    lo,hi=ranges(seg_row,bq,bk)
    return pl.pallas_call(functools.partial(bwd_kernel,bq,bk,sub),
      out_shape=(jax.ShapeDtypeStruct((chunks,192,width),jnp.bfloat16),jax.ShapeDtypeStruct((192,full),jnp.bfloat16)),
      in_specs=[SM,SM,VM,VM,VM,VM,VM,VM,VM],out_specs=(VM,VM),
      scratch_shapes=[pltpu.VMEM((full,128),jnp.bfloat16),pltpu.VMEM((80,full),jnp.bfloat16),pltpu.VMEM((full,128),jnp.bfloat16),
        pltpu.VMEM((80,full),jnp.bfloat16),pltpu.VMEM((full,128),jnp.bfloat16),pltpu.VMEM((128,full),jnp.bfloat16),pltpu.VMEM((128,full),jnp.float32)],
      compiler_params=pltpu.CompilerParams(vmem_limit_bytes=56<<20),
      cost_estimate=pl.CostEstimate(flops=1580*full*full,bytes_accessed=16<<20,transcendentals=0),
      name="attend_bwd")(lo,hi,qkv,seg_row[None,:],do,raw,lse,cos,sin)

FF = 2624
BLOCK_ORDER = 64
rope_base = 160000.0
norm_eps = 1e-05
adam_eps = 1e-08
beta_one = 0.5
beta_two = 0.5
block_rate = 0.03
gain_rate = 0.75
decay_rate = 0.01
BF = jnp.bfloat16
F32 = jnp.float32


def layer_norm(values, gain_row):
    center = values - jnp.mean(values, axis=-1, keepdims=True)
    spread = jnp.mean(center * center, axis=-1, keepdims=True)
    return center * lax.rsqrt(spread + norm_eps) * gain_row


def norm_back(values, gain_row, grad_rows):
    unused, pullback = jax.vjp(layer_norm, values, gain_row)
    return pullback(grad_rows)


def doc_positions(seg_row):
    doc_ids = jnp.arange(NDOC, dtype=jnp.int32)
    matches = seg_row[:, None] == doc_ids[None, :]
    counts = jnp.sum(matches.astype(jnp.int32), axis=0)
    starts = jnp.cumsum(counts) - counts
    doc_begin = jnp.sum(jnp.where(matches, starts[None, :], 0), axis=1)
    return jnp.arange(seg_row.shape[0], dtype=jnp.int32) - doc_begin


def rope_tables(positions):
    half = HEAD // 2
    frequency = rope_base ** (-(jnp.arange(half, dtype=F32) * 2.0) / HEAD)
    angles = positions.astype(F32)[None, :] * frequency[:, None]
    return jnp.cos(angles), jnp.sin(angles)


def gated_gelu(gate_up):
    return jax.nn.gelu(gate_up[:, :FF], approximate=False) * gate_up[:, FF:]


def gated_both(gate_up, grad_hidden):
    hidden, pullback = jax.vjp(gated_gelu, gate_up)
    return hidden, pullback(grad_hidden)[0]


def mm(a, b, da, db):
    return lax.dot_general(a, b, (((da,), (db,)), ((), ())), preferred_element_type=F32)


def after(x, *others):
    return lax.optimization_barrier((x, *others))[0]


def swap_bit(x, axis, bit):
    n = lax.axis_size(axis)
    return lax.ppermute(x, axis, [(s, s ^ bit) for s in range(n)])


def two_parts():
    return lax.axis_size("fsdp") == 2 and lax.axis_size("ctx") % 2 == 0


def own_piece(shard):
    half = shard.shape[0] // 2
    return lax.dynamic_slice_in_dim(shard, (lax.axis_index("ctx") % 2) * half, half)


def joined(shard, got, twin):
    first = lax.axis_index("ctx") % 2 == 0
    mine = lax.axis_index("fsdp") == 0
    other = jnp.concatenate([jnp.where(first, got, twin), jnp.where(first, twin, got)], axis=0)
    return jnp.concatenate([jnp.where(mine, shard, other), jnp.where(mine, other, shard)], axis=0)


def halving_applies():
    return lax.axis_size("ctx") == 16 and lax.axis_size("fsdp") == 2


def half_of(x, axis, bit):
    return lax.dynamic_index_in_dim(x, bit, axis, keepdims=False)


def sum_all(x):
    for name in ("ctx", "fsdp"):
        for b in range(lax.axis_size(name).bit_length() - 1):
            x = x + swap_bit(x, name, 1 << b)
    return x


def scatter_kernel(counts, parts, where_ref, *refs):
    n = len(counts)
    grads, outs, stage, sems = refs[:n], refs[n : n + parts], refs[n + parts], refs[n + parts + 1]
    lane = lax.broadcasted_iota(jnp.int32, (32, 128), 1) < 64
    size = outs[0].shape[0]
    base = 0
    for grad, (row_tiles, col_tiles) in zip(grads, counts):

        def drain(buf):
            pltpu.make_async_copy(
                stage.at[buf, pl.ds(0, col_tiles)], outs[0].at[pl.ds(0, col_tiles)], sems.at[buf]
            ).wait()

        def strip(i, carry, grad=grad, base=base, col_tiles=col_tiles, drain=drain):
            buf = lax.rem(i, 2)

            @pl.when(i >= 2)
            def _():
                drain(buf)

            top = pl.ds(pl.multiple_of(i * 64, 64), 32)
            bottom = pl.ds(pl.multiple_of(i * 64 + 32, 32), 32)
            for j in range(col_tiles // 2):
                a = grad[top, j * 128 : (j + 1) * 128].astype(F32)
                b = grad[bottom, j * 128 : (j + 1) * 128].astype(F32)
                stage[buf, 2 * j] = jnp.where(lane, a, pltpu.roll(b, 64, 1)).astype(BF)
                stage[buf, 2 * j + 1] = jnp.where(lane, pltpu.roll(a, 64, 1), b).astype(BF)
            for j in range(col_tiles):
                place = where_ref[base + i * col_tiles + j]
                if parts == 1:
                    pltpu.make_async_copy(stage.at[buf, j], outs[0].at[place], sems.at[buf]).start()
                else:

                    @pl.when(place < size)
                    def _(j=j, place=place):
                        pltpu.make_async_copy(stage.at[buf, j], outs[0].at[place], sems.at[buf]).start()

                    @pl.when(place >= size)
                    def _(j=j, place=place):
                        pltpu.make_async_copy(stage.at[buf, j], outs[1].at[place - size], sems.at[buf]).start()

            return carry

        lax.fori_loop(0, row_tiles, strip, 0)
        drain((row_tiles - 2) % 2)
        drain((row_tiles - 1) % 2)
        base += row_tiles * col_tiles


def scatter_tiles(grads, where, total, parts):
    counts = tuple((g.shape[0] // 64, g.shape[1] // 64) for g in grads)
    widest = max(c for _, c in counts)
    return pl.pallas_call(
        functools.partial(scatter_kernel, counts, parts),
        out_shape=(jax.ShapeDtypeStruct((total // parts, 32, 128), BF),) * parts,
        in_specs=[SM] + [VM] * len(grads),
        out_specs=(pl.BlockSpec(memory_space=pl.ANY),) * parts,
        scratch_shapes=[pltpu.VMEM((2, widest, 32, 128), BF), pltpu.SemaphoreType.DMA((2,))],
        compiler_params=pltpu.CompilerParams(vmem_limit_bytes=48 << 20),
        cost_estimate=pl.CostEstimate(flops=40 << 30, bytes_accessed=40 << 20, transcendentals=0),
        name="scatter_tiles",
    )(where, *grads)


def soap_kernel(block, kind_ref, row_ref, col_ref, odd_ref, live_ref, qkv, early, master, first, second, left, right,
                grads_out, master_out, copy_out, first_out, second_out, tiles, sem):
    step = pl.program_id(0)
    total = tiles.shape[0]

    @pl.when(step == 0)
    def _():
        def fetch(n, carry):
            rows = pl.ds(pl.multiple_of(row_ref[n], 64), 64)
            cols = pl.ds(pl.multiple_of(col_ref[n], 128), 128)

            pltpu.make_async_copy(qkv.at[rows, cols], tiles.at[n], sem).start()
            return carry

        lax.fori_loop(0, total, fetch, 0)
        pltpu.make_async_copy(tiles, tiles, sem).wait()

    def two(v):
        hi = v.astype(BF)
        return hi, (v - hi.astype(F32)).astype(BF)

    def product(a, b):
        ah, al = two(a)
        bh, bl = two(b)
        return jnp.dot(
            jnp.concatenate([ah, ah, al], axis=1), jnp.concatenate([bh, bl, bh], axis=0), preferred_element_type=F32
        )

    def each(f, *lists):
        return [f(*row) for row in zip(*lists)]

    for low in range(0, block, 8):
        group = range(low, min(low + 8, block))

        def own_tile(k):
            n = jnp.minimum(step * block + k, total - 1)
            pair = tiles[n].astype(F32)
            turned = jnp.where(odd_ref[n] == 1, pair[:, 64:128], pair[:, 0:64]).T
            flat = early[k].astype(F32)
            tile = jnp.where(kind_ref[n] != 0, turned, jnp.concatenate([flat[:, 0:64], flat[:, 64:128]], axis=0))
            return jnp.where(live_ref[n] != 0, tile, 0.0)

        lives = [live_ref[jnp.minimum(step * block + k, total - 1)] != 0 for k in group]
        tile_list = [own_tile(k) for k in group]
        half = each(lambda k, t: product(left[k].T, t), group, tile_list)
        turned = each(lambda k, t: product(t, right[k]), group, half)
        firsts = each(lambda k, t: beta_one * first[k] + (1.0 - beta_one) * t, group, turned)
        seconds = each(lambda k, t: beta_two * second[k] + (1.0 - beta_two) * t * t, group, turned)
        normal = each(lambda f, s: f / (jnp.sqrt(s) + adam_eps), firsts, seconds)
        half = each(lambda k, t: product(left[k], t), group, normal)
        restored = each(lambda k, t: product(t, right[k].T), group, half)
        for k, live, tile, f, s, r in zip(group, lives, tile_list, firsts, seconds, restored):
            weights = master[k]
            new = jnp.where(live, weights - block_rate * (r + decay_rate * weights), weights)
            grads_out[k] = tile
            master_out[k] = new
            copy_out[k] = new.astype(BF)
            first_out[k] = jnp.where(live, f, first[k])
            second_out[k] = jnp.where(live, s, second[k])


def soap_step(picks, qkv, early, master, first, second, left, right):
    cap = master.shape[0]
    block = min(16, cap)
    spec = pl.BlockSpec((block, 64, 64), lambda i: (i, 0, 0))
    whole = pl.BlockSpec(memory_space=pl.ANY)
    like = jax.ShapeDtypeStruct(master.shape, F32)
    return pl.pallas_call(
        functools.partial(soap_kernel, block),
        grid=(-(-cap // block),),
        out_shape=(like, like, jax.ShapeDtypeStruct(master.shape, BF), like, like),
        in_specs=[SM] * 5 + [whole, pl.BlockSpec((block, 32, 128), lambda i: (i, 0, 0))] + [spec] * 5,
        out_specs=(spec,) * 5,
        scratch_shapes=[pltpu.VMEM((cap, 64, 128), BF), pltpu.SemaphoreType.DMA],
        compiler_params=pltpu.CompilerParams(vmem_limit_bytes=40 << 20),
        cost_estimate=pl.CostEstimate(flops=1 << 30, bytes_accessed=30 << 20, transcendentals=0),
        name="soap",
    )(*picks, qkv, early, master, first, second, left, right)


def own_picks(slot_table, slot_cap, heads):
    device_index = lax.axis_index(("ctx", "fsdp"))
    own_ids = device_index * slot_cap + jnp.arange(slot_cap, dtype=jnp.int32)
    hit = slot_table[None, :] == own_ids[:, None]
    live = jnp.any(hit, axis=1).astype(jnp.int32)
    tile = jnp.sum(jnp.where(hit, jnp.arange(slot_table.shape[0], dtype=jnp.int32)[None, :], 0), axis=1)
    across = heads * HEAD // 64
    is_qkv = tile < 3 * across * across
    q_row, q_col = tile // (3 * across), tile % (3 * across)
    row = jnp.where(is_qkv, (q_col % across) * 3 + q_col // across, 0)
    col = jnp.where(is_qkv, q_row, 0)
    return is_qkv.astype(jnp.int32), row * 64, (col // 2) * 128, col % 2, live


def gain_step(grads_in, gains_old, first_old, second_old):
    first_new = beta_one * first_old + (1.0 - beta_one) * grads_in
    second_new = beta_two * second_old + (1.0 - beta_two) * grads_in * grads_in
    gains_new = gains_old - gain_rate * first_new / (jnp.sqrt(second_new) + adam_eps)
    return (gains_new, first_new, second_new)


def on_device(
    inputs,
    cotangent,
    segments,
    w_qkv,
    w_out,
    w_in,
    w_down,
    norm_gains,
    slot_table,
    master,
    first_moment,
    rotated_second_moments,
    row_eigenbasis,
    column_eigenbasis,
    gain_master,
    gain_first,
    gain_second,
):
    micro, shard, width = inputs.shape
    heads = width // HEAD
    full_len = segments.shape[1]
    ctx_size = lax.axis_size("ctx")
    ctx_index = lax.axis_index("ctx")
    copies = max(1, ctx_size // heads)

    def spread(x):
        if copies > 1:
            x = jnp.repeat(x, copies, axis=0)
        return lax.all_to_all(x, "ctx", 0, 0, tiled=True)

    def collect(x):
        x = lax.all_to_all(x, "ctx", 0, 0, tiled=True)
        return x[::copies] if copies > 1 else x

    gains = lax.all_gather(norm_gains, "fsdp", axis=1, tiled=True).astype(F32)
    fast_gather = two_parts()
    if fast_gather:
        got_qkv = swap_bit(own_piece(w_qkv), "fsdp", 1)
        full_qkv = joined(w_qkv, got_qkv, swap_bit(got_qkv, "ctx", 1))
        later = [w_out, w_in, w_down]
        got_later = [swap_bit(after(own_piece(w), got_qkv), "fsdp", 1) for w in later]
    else:
        full_qkv, full_out, full_in, full_down = (
            lax.all_gather(w, "fsdp", axis=0, tiled=True) for w in (w_qkv, w_out, w_in, w_down)
        )

    qkv_all, tables, normed_all, layer_ins, sends = [], [], [], [], []
    for b in range(micro):
        seg_all = segments[b]
        positions = doc_positions(seg_all)
        tables.append(positions)
        own_cos, own_sin = rope_tables(lax.dynamic_slice_in_dim(positions, ctx_index * shard, shard))
        layer_in = inputs[b].astype(F32)
        normed = layer_norm(layer_in, gains[0]).astype(BF)
        proj = mm(full_qkv, normed, 0, 1).reshape(3, heads, HEAD, shard)

        def rotate(v, scale):
            a, c = v[:, : HEAD // 2], v[:, HEAD // 2 :]
            return jnp.concatenate([a * own_cos - c * own_sin, c * own_cos + a * own_sin], axis=1) * scale

        send = jnp.concatenate(
            [rotate(proj[0], LOG2E * HEAD**-0.5).astype(BF), rotate(proj[1], 1.0).astype(BF), proj[2].astype(BF)],
            axis=1,
        )
        sends.append(send)
        qkv_all.append(spread(send))
        normed_all.append(normed)
        layer_ins.append(layer_in)

    tables = [rope_tables(after(p, *sends)) for p in tables]
    attended_all, raw_all, outs = [], [], []
    for b in range(micro):
        ready = after(qkv_all[b], *(outs[-1:] or sends))
        out, raw, lse = attend_forward(ready, segments[b], bq=min(1024, full_len), bk=512, sub=min(1024, full_len))
        outs.append(out)
        raw_all.append((raw, lse))
        attended_all.append(collect(out).reshape(width, shard))
    wide = lax.all_gather(after(jnp.stack(normed_all), qkv_all[-1]), "ctx", axis=1, tiled=True)
    normed_wide = [wide[b] for b in range(micro)]
    if fast_gather:
        got_later = [after(g, outs[0]) for g in got_later]
        twins = [after(swap_bit(g, "ctx", 1), outs[-1]) for g in got_later]
        full_out, full_in, full_down = (joined(*parts) for parts in zip(later, got_later, twins))

    outputs_list, d_middles, d_att_all = [], [], []
    hidden_all, d_gate_all, normed_two_all, branch_all = [], [], [], []
    gain_two_sum = 0.0
    for b in range(micro):
        if b:
            attended_all[b] = after(attended_all[b], branch_all[b - 1])
        middle_value = layer_ins[b] + mm(attended_all[b], full_out, 0, 0)
        normed_two = layer_norm(middle_value, gains[1]).astype(BF)
        gate_up = mm(normed_two, full_in, 1, 0)
        grad_top = cotangent[b]
        d_hidden = mm(grad_top, full_down, 1, 1)
        hidden, d_gate_up = gated_both(gate_up, d_hidden)
        hidden, d_gate_up = hidden.astype(BF), d_gate_up.astype(BF)
        result = middle_value + mm(hidden, full_down, 1, 0)
        outputs_list.append(result.astype(BF))
        d_normed_two = mm(d_gate_up, full_in, 1, 1)
        d_mid_norm, gain_two = norm_back(middle_value, gains[1], d_normed_two)
        d_middle = grad_top.astype(F32) + d_mid_norm
        grad_branch = d_middle.astype(BF)
        d_att = mm(full_out, grad_branch, 1, 1).astype(BF).reshape(heads, HEAD, shard)
        d_att_all.append(spread(d_att))
        d_middles.append(d_middle)
        hidden_all.append(hidden)
        d_gate_all.append(d_gate_up)
        normed_two_all.append(normed_two)
        branch_all.append(grad_branch)
        gain_two_sum = gain_two_sum + gain_two

    def rows(parts):
        return jnp.concatenate(parts, axis=0)

    grad_out = mm(jnp.concatenate(attended_all, axis=1), rows(branch_all), 1, 0).astype(BF)
    grad_in = mm(rows(normed_two_all), rows(d_gate_all), 0, 0).astype(BF)
    grad_down = mm(rows(hidden_all), cotangent.reshape(-1, width), 0, 0).astype(BF)
    slot_cap = master.shape[0]
    slot_total = slot_cap * ctx_size * lax.axis_size("fsdp")
    where = after(slot_table[3 * (width // 64) ** 2 :], d_att_all[0])
    fast = halving_applies() and micro == 2
    waits = [()] * micro
    if fast:
        owner = where // slot_cap
        rest = where % slot_cap
        cut = slot_cap // 2
        low = rest < cut
        core = (owner // 2) % 2
        x_rel = (owner % 2) ^ lax.axis_index("fsdp")
        ctx_rel = (owner // 2) ^ ctx_index
        y_rel, z_one, z_two = (ctx_rel // 2) % 2, (ctx_rel // 4) % 2, ctx_rel // 8
        z_rel = z_one * 2 + z_two
        place = jnp.where(
            low,
            ((x_rel * 2 + y_rel) * 4 + z_rel) * cut + rest,
            16 * cut + ((y_rel * 2 + x_rel) * 4 + z_rel) * (slot_cap - cut) + rest - cut,
        )
        where = place + jnp.where(core == ctx_index % 2, slot_total // 2, 0)
        send, keep = scatter_tiles([grad_out, grad_in, grad_down], where, slot_total, 2)
        got = swap_bit(send, "ctx", 1)

        def both(low, high):
            return keep[low:high] + got[low:high]

        ours = [both(0, 8 * cut), both(16 * cut, 16 * cut + 8 * (slot_cap - cut))]
        theirs = [both(8 * cut, 16 * cut), both(16 * cut + 8 * (slot_cap - cut), 16 * slot_cap)]
        near = [swap_bit(theirs[0], "fsdp", 1), swap_bit(theirs[1], "ctx", 2)]
        waits[0] = (*ours, *theirs)
    else:
        (slotted,) = scatter_tiles([grad_out, grad_in, grad_down], where, slot_total, 1)
        own_slots = lax.psum_scatter(slotted, ("ctx", "fsdp"), scatter_dimension=0, tiled=True)

    d_proj_all, grad_heads = [], 0.0
    for b in range(micro):
        cosine, sine = tables[b]
        d_att = after(d_att_all[b], *waits[b])
        grads, flat = attend_backward(
            qkv_all[b], segments[b], d_att, *raw_all[b], cosine, sine, bq=512, bk=512, sub=512
        )
        if fast and b == 0:
            near = [after(v, grads) for v in near]
            next_ours = [t[: t.shape[0] // 2] + v[: t.shape[0] // 2] for t, v in zip(ours, near)]
            next_theirs = [t[t.shape[0] // 2 :] + v[t.shape[0] // 2 :] for t, v in zip(ours, near)]
            next_near = [swap_bit(next_theirs[0], "ctx", 2), swap_bit(next_theirs[1], "fsdp", 1)]
            waits[1] = (*next_ours, *next_theirs)
        elif fast:
            next_near = [after(v, grads) for v in next_near]
            pair = [(t.reshape(2, 2, -1, 32, 128), v.reshape(2, 2, -1, 32, 128)) for t, v in zip(next_ours, next_near)]
            kept, sent = (jnp.concatenate([t[side] + v[side] for t, v in pair], axis=1) for side in (0, 1))
            got = swap_bit(sent, "ctx", 4)
            kept, sent = (kept[side] + got[side] for side in (0, 1))
            own_slots = kept + swap_bit(sent, "ctx", 8)
        d_proj_all.append(collect(grads))
        grad_heads = grad_heads + mm(flat, normed_wide[b], 1, 0)

    grad_heads = after(grad_heads.astype(BF), d_proj_all[0], *(next_near if fast else ()))
    if lax.axis_size("fsdp") == 2:
        grad_heads = grad_heads + swap_bit(grad_heads, "fsdp", 1)
    else:
        grad_heads = lax.psum(grad_heads, "fsdp")
    grad_qkv = lax.all_gather(grad_heads[None], "ctx", axis=0, tiled=True)[::copies].reshape(3 * width, width)

    input_grads = []
    gain_one_sum = 0.0
    for b in range(micro):
        d_proj = d_proj_all[b].reshape(heads, 3, HEAD, shard).transpose(1, 0, 2, 3).reshape(3 * width, shard)
        d_normed = mm(d_proj, full_qkv, 0, 1)
        d_in_norm, gain_one = norm_back(layer_ins[b], gains[0], d_normed)
        input_grads.append((d_middles[b] + d_in_norm).astype(BF))
        gain_one_sum = gain_one_sum + gain_one
    gain_grads = sum_all(jnp.stack([gain_one_sum, gain_two_sum]))

    picks = own_picks(slot_table, slot_cap, heads)
    own_grads, new_master, new_copy, new_first, new_second = soap_step(
        picks, grad_qkv, own_slots, master, first_moment, rotated_second_moments, row_eigenbasis, column_eigenbasis
    )
    new_gains, new_gain_first, new_gain_second = gain_step(gain_grads, gain_master, gain_first, gain_second)
    return (
        jnp.stack(outputs_list),
        jnp.stack(input_grads),
        own_grads,
        gain_grads,
        new_master,
        new_copy,
        new_first,
        new_second,
        new_gains,
        new_gain_first,
        new_gain_second,
    )


def solution(mesh):
    tokens = P("fsdp", "ctx", None)
    slots = P(("ctx", "fsdp"), None, None)
    placed = (
        tokens,
        tokens,
        *(P("fsdp", None),) * 5,
        P(None, "fsdp"),
        P(),
        *(slots,) * 5,
        *(P(),) * 3,
    )
    return jax.shard_map(
        on_device,
        mesh=mesh,
        in_specs=placed,
        out_specs=(tokens, tokens, slots, P(), slots, slots, slots, slots, P(), P(), P()),
        check_vma=False,
    )
```

profile of v0, /device:TPU:0, one launch (start us, length us, event | category | flops | bytes accessed | tf_op | source)
XLA Modules:
  0.0 1026.3 jit_solution(4414778282163772935)
XLA Ops:
  13.8 33.9 %all_gather.9 = bf16[2,1024]{1,0:T(2,128)(2,1)S(1)} all-gather(bf16[2,512]{1,0:T(2,128)(2,1)S(1)} %copy-done.101), channel_id=1, replica_groups=mesh['ctx'=16,'fsdp'=2] {'fsdp'}, dimensions={1}, use_global_device_ids=true | all-gather | bytes 6144 | tf_op jit(solution)/shard_map/all_gather | solution.py:470
  62.6 6.5 all-to-all-start
  93.7 34.8 %all-to-all-done.qkv_ref = bf16[16,192,512]{2,1,0:T(8,128)(2,1)S(1)} async-done(((bf16[16,192,512]{2,1,0:T(8,128)(2,1)}), bf16[16,192,512]{2,1,0:T(8,128)(2,1)S(1)}, u32[]{:S(2)}, u32[]{:S(2)}) %all-to-all-start) | async-done | bytes 3145760 | tf_op jit(solution)/shard_map/all_to_all | solution.py:464
  128.5 15.5 %all-to-all-start.2 = ((bf16[16,192,512]{2,1,0:T(8,128)(2,1)}), bf16[16,192,512]{2,1,0:T(8,128)(2,1)}, u32[]{:S(2)}, u32[]{:S(2)}) async-start(bf16[16,192,512]{2,1,0:T(8,128)(2,1)} %pad_maximum_fusion.6), calls=%async_computation.2 | async-start | bytes 6291456 | tf_op jit(solution)/shard_map/all_to_all | solution.py:464
  143.9 48.7 %attend_fwd.2 = (bf16[16,64,512]{2,1,0:T(8,128)(2,1)S(1)}, f32[64,8192]{1,0:T(8,128)S(1)}, f32[1,8192]{1,0:T(1,128)S(1)}) custom-call(s32[8]{0:T(128)S(1)} %get-tuple-element.245.lo_ref, s32[8]{0:T(128)S(1)} %get-tuple-element.246.hi_ref, bf16[16,192,512]{2,1,0:T(8,128)(2,1)S(1)} %all-to-all-done.qkv_ref, s32[1,8192]{1,0:T(1,128)S(1)} %get-tuple-element.214.seg_ref), custom_call_target="tpu_custom_call" | custom-call | flops 76504104960 | bytes 8388608 | tf_op jit(solution)/shard_map/attend_fwd/pallas_call | solution.py:157
  195.9 7.5 all-to-all-done.2.qkv_ref
  203.4 15.5 %all-to-all-start.1 = ((bf16[16,64,512]{2,1,0:T(8,128)(2,1)}), bf16[16,64,512]{2,1,0:T(8,128)(2,1)}, u32[]{:S(2)}, u32[]{:S(2)}) async-start(bf16[16,64,512]{2,1,0:T(8,128)(2,1)} %copy-done.6), calls=%async_computation.1 | async-start | bytes 2097152 | tf_op jit(solution)/shard_map/all_to_all | solution.py:467
  219.6 68.4 %attend_fwd.3 = (bf16[16,64,512]{2,1,0:T(8,128)(2,1)}, f32[64,8192]{1,0:T(8,128)S(1)}, f32[1,8192]{1,0:T(1,128)S(1)}) custom-call(s32[8]{0:T(128)S(1)} %get-tuple-element.239.lo_ref, s32[8]{0:T(128)S(1)} %get-tuple-element.240.hi_ref, bf16[16,192,512]{2,1,0:T(8,128)(2,1)} %all-to-all-done.2.qkv_ref, s32[1,8192]{1,0:T(1,128)S(1)} %get-tuple-element.215.seg_ref), custom_call_target="tpu_custom_call" | custom-call | flops 76504104960 | bytes 8388608 | tf_op jit(solution)/shard_map/attend_fwd/pallas_call | solution.py:157
  318.8 8.2 fusion.142
  327.0 13.5 %multiply_convert_fusion.1 = (bf16[512,2624]{1,0:T(8,128)(2,1)}, f32[512,2624]{1,0:T(8,128)S(1)}) fusion(f32[512,5248]{1,0:T(8,128)S(1)} %fusion.142), kind=kLoop, calls=%fused_computation.39 | loop fusion | flops 88670208 | bytes 18808832 | tf_op jit(solution)/shard_map/convert_element_type | solution.py:532
  340.5 13.2 %bitcast_multiply_fusion.3 = (f32[512,2624]{1,0:T(8,128)}, f32[512,2624]{1,0:T(8,128)}) fusion(f32[512,2624]{1,0:T(8,128)S(1)} %get-tuple-element.159, f32[512,5248]{1,0:T(8,128)} %copy-done.28, bf16[2,512,1024]{2,1,0:T(8,128)(2,1)S(1)} %copy-done.29, bf16[1312,1024]{1,0:T(8,128)(2,1)} %get-tuple-element.183, bf16[1312,1024]{1,0:T(8,128)(2,1)} %get-tuple-element.182), kind=kOutput, calls=%fused_computation.23 | convolution fusion | flops 2783707136 | bytes 33423360 | tf_op jit(solution)/shard_map/dot_general | solution.py:227
  353.7 8.0 add_convert_fusion.1
  361.7 14.6 %multiply_reduce_fusion.1 = (f32[1024]{0:T(1024)}, f32[512]{0:T(512)S(1)}, f32[512,1024]{1,0:T(8,128)}) fusion(f32[512,1024]{1,0:T(8,128)} %copy-done.18, f32[512]{0:T(512)S(1)} %fusion.120, f32[512]{0:T(512)S(1)} %broadcast_multiply_fusion.1, f32[1024]{0:T(1024)S(1)} %bitcast.200, bf16[512,5248]{1,0:T(8,128)(2,1)} %add_convert_fusion.1, ...), kind=kOutput, calls=%fused_computation.137 | convolution fusion | flops 5528091136 | bytes 20330496 | tf_op jit(solution)/shard_map/dot_general | solution.py:227
  385.3 6.3 all-to-all-start.4
  397.2 9.2 fusion.140
  406.4 18.2 %bitcast_multiply_fusion.1 = (f32[512,2624]{1,0:T(8,128)}, f32[512,2624]{1,0:T(8,128)S(1)}, f32[2624,512]{0,1:T(8,128)}) fusion(f32[512,5248]{1,0:T(8,128)S(1)} %fusion.140, bf16[2,512,1024]{2,1,0:T(8,128)(2,1)S(1)} %copy-done.31, bf16[1312,1024]{1,0:T(8,128)(2,1)} %get-tuple-element.183, bf16[1312,1024]{1,0:T(8,128)(2,1)S(1)} %copy-done.53), kind=kOutput, calls=%fused_computation.21 | convolution fusion | flops 2849538048 | bytes 28049408 | tf_op jit(solution)/shard_map/dot_general | solution.py:227
  424.6 7.3 multiply_add_fusion
  432.0 8.1 add_convert_fusion
  440.1 11.6 %multiply_reduce_fusion = (f32[1024]{0:T(1024)}, f32[512]{0:T(512)S(1)}, f32[512,1024]{1,0:T(8,128)S(1)}) fusion(f32[512,1024]{1,0:T(8,128)S(1)} %copy-done.22, f32[512]{0:T(512)S(1)} %fusion.121, f32[512]{0:T(512)S(1)} %broadcast_multiply_fusion, f32[1024]{0:T(1024)S(1)} %bitcast.203, bf16[512,5248]{1,0:T(8,128)(2,1)} %add_convert_fusion, ...), kind=kOutput, calls=%fused_computation.136 | convolution fusion | flops 5528091136 | bytes 20330496 | tf_op jit(solution)/shard_map/dot_general | solution.py:227
  454.9 18.8 %convolution_convert_fusion.refs_1_ = bf16[1024,5248]{1,0:T(8,128)(2,1)} fusion(bf16[512,5248]{1,0:T(8,128)(2,1)} %add_convert_fusion, bf16[512,5248]{1,0:T(8,128)(2,1)} %add_convert_fusion.1, bf16[512,1024]{1,0:T(8,128)(2,1)S(1)} %copy-done.65, bf16[512,1024]{1,0:T(8,128)(2,1)S(1)} %copy-done.63), kind=kOutput, calls=%fused_computation.4 | convolution fusion | flops 11036917760 | bytes 23592960 | tf_op jit(solution)/shard_map/dot_general | solution.py:227
  478.1 7.8 convolution_convert_fusion.1.refs_2_
  486.0 39.0 %scatter_tiles.1 = (bf16[1504,32,128]{2,1,0:T(8,128)(2,1)}, bf16[1504,32,128]{2,1,0:T(8,128)(2,1)}) custom-call(s32[2224]{0:T(1024)S(1)} %select_add_fusion.where_ref, bf16[1024,1024]{1,0:T(8,128)(2,1)S(1)} %fusion.64.refs_0_, bf16[1024,5248]{1,0:T(8,128)(2,1)} %convolution_convert_fusion.refs_1_, bf16[2624,1024]{1,0:T(8,128)(2,1)} %convolution_convert_fusion.1.refs_2_), custom_call_target="tpu_custom_call" | custom-call | flops 42949672960 | bytes 41943040 | tf_op jit(solution)/shard_map/scatter_tiles/pallas_call | solution.py:322
  527.5 8.9 multiply_sine_fusion
  544.5 11.4 %slice_add_fusion = (bf16[376,32,128]{2,1,0:T(8,128)(2,1)}, bf16[376,32,128]{2,1,0:T(8,128)(2,1)}, bf16[376,32,128]{2,1,0:T(8,128)(2,1)S(1)}, bf16[376,32,128]{2,1,0:T(8,128)(2,1)S(1)}) fusion(bf16[1504,32,128]{2,1,0:T(8,128)(2,1)} %collective-permute-done.8, bf16[1504,32,128]{2,1,0:T(8,128)(2,1)} %get-tuple-element.66), kind=kLoop, calls=%fused_computation.77 | loop fusion | flops 6160384 | bytes 36962304 | tf_op jit(solution)/shard_map/add | solution.py:579
  557.8 82.6 %attend_bwd.2 = (bf16[16,192,512]{2,1,0:T(8,128)(2,1)}, bf16[192,8192]{1,0:T(8,128)(2,1)}) custom-call(s32[16]{0:T(128)} %get-tuple-element.243.lo_ref, s32[16]{0:T(128)} %get-tuple-element.244.hi_ref, bf16[16,192,512]{2,1,0:T(8,128)(2,1)} %copy-done, s32[1,8192]{1,0:T(1,128)} %copy-done.8, bf16[16,64,512]{2,1,0:T(8,128)(2,1)} %all-to-all-done.4.do_ref, ...), custom_call_target="tpu_custom_call" | custom-call | flops 106032005120 | bytes 16777216 | tf_op jit(solution)/shard_map/attend_bwd/pallas_call | solution.py:167
  652.5 6.2 all-to-all-start.5
  658.7 105.2 %attend_bwd.3 = (bf16[16,192,512]{2,1,0:T(8,128)(2,1)}, bf16[192,8192]{1,0:T(8,128)(2,1)}) custom-call(s32[16]{0:T(128)} %get-tuple-element.241.lo_ref, s32[16]{0:T(128)} %get-tuple-element.242.hi_ref, bf16[16,192,512]{2,1,0:T(8,128)(2,1)} %all-to-all-done.2.qkv_ref, s32[1,8192]{1,0:T(1,128)} %copy-done.7, bf16[16,64,512]{2,1,0:T(8,128)(2,1)} %copy-done.66, ...), custom_call_target="tpu_custom_call" | custom-call | flops 106032005120 | bytes 16777216 | tf_op jit(solution)/shard_map/attend_bwd/pallas_call | solution.py:167
  763.9 8.6 fusion
  772.6 10.1 fusion.74
  837.3 76.1 %collective-permute-done.14 = bf16[2,94,32,128]{3,2,1,0:T(8,128)(2,1)S(1)} collective-permute-done((bf16[2,94,32,128]{3,2,1,0:T(8,128)(2,1)S(1)}, bf16[2,94,32,128]{3,2,1,0:T(8,128)(2,1)S(1)}, u32[]{:S(2)}, u32[]{:S(2)}) %collective-permute-start.14) | collective-permute-done | bytes 1540128 | tf_op jit(solution)/shard_map/ppermute | solution.py:236
  931.4 19.3 %collective-permute-done.15 = bf16[94,32,128]{2,1,0:T(8,128)(2,1)S(1)} collective-permute-done((bf16[94,32,128]{2,1,0:T(8,128)(2,1)S(1)}, bf16[94,32,128]{2,1,0:T(8,128)(2,1)S(1)}, u32[]{:S(2)}, u32[]{:S(2)}) %collective-permute-start.15) | collective-permute-done | bytes 770080 | tf_op jit(solution)/shard_map/ppermute | solution.py:236
  969.2 27.7 %soap.1 = (f32[94,64,64]{2,1,0:T(8,128)S(1)}, f32[94,64,64]{2,1,0:T(8,128)S(1)}, bf16[94,64,64]{2,1,0:T(8,128)(2,1)S(1)}, f32[94,64,64]{2,1,0:T(8,128)S(1)}, f32[94,64,64]{2,1,0:T(8,128)}) custom-call(s32[94]{0:T(128)S(1)} %fusion.132.kind_ref, s32[94]{0:T(128)S(1)} %get-tuple-element.226.row_ref, s32[94]{0:T(128)S(1)} %fusion.131.col_ref, ...), custom_call_target="tpu_custom_call" | custom-call | flops 1073741824 | bytes 31457280 | tf_op jit(solution)/shard_map/soap/pallas_call | solution.py:401
  (400 shorter events, 239.8 us)
Async XLA Ops:
  10.0 38.1 %collective-permute-start = (bf16[256,3072]{1,0:T(8,128)(2,1)}, bf16[256,3072]{1,0:T(8,128)(2,1)}, u32[]{:S(2)}, u32[]{:S(2)}) collective-permute-start(bf16[256,3072]{1,0:T(8,128)(2,1)} %constant_dynamic-slice_fusion.3), channel_id=1, source_target_pairs={{0,1},{1,0},{2,3},{3,2},{4,5},{5,4},{6,7},{7,6},{8,9},{9,8},{10,11... | collective-permute-start | bytes 4718600 | tf_op jit(solution)/shard_map/ppermute | solution.py:236
  13.0 513.0 %copy-start.7 = (s32[1,8192]{1,0:T(1,128)}, s32[1,8192]{1,0:T(1,128)S(1)}, u32[]{:S(2)}) copy-start(s32[1,8192]{1,0:T(1,128)S(1)} %get-tuple-element.215.seg_ref) | copy-start | bytes 98308
  48.1 3.7 collective-permute-start.1
  62.6 65.9 %all-to-all-start = ((bf16[16,192,512]{2,1,0:T(8,128)(2,1)}), bf16[16,192,512]{2,1,0:T(8,128)(2,1)S(1)}, u32[]{:S(2)}, u32[]{:S(2)}) async-start(bf16[16,192,512]{2,1,0:T(8,128)(2,1)} %pad_maximum_fusion.5), calls=%async_computation | async-start | bytes 6291456 | tf_op jit(solution)/shard_map/all_to_all | solution.py:464
  81.0 114.5 %collective-permute-start.6 = (bf16[656,1024]{1,0:T(8,128)(2,1)}, bf16[656,1024]{1,0:T(8,128)(2,1)}, u32[]{:S(2)}, u32[]{:S(2)}) collective-permute-start(bf16[656,1024]{1,0:T(8,128)(2,1)} %constant_dynamic-slice_fusion), channel_id=1, source_target_pairs={{0,1},{1,0},{2,3},{3,2},{4,5},{5,4},{6,7},{7,6},{8,9},{9,8},{10,11... | collective-permute-start | bytes 4030472 | tf_op jit(solution)/shard_map/ppermute | solution.py:236
  82.5 136.4 %collective-permute-start.4 = (bf16[256,5248]{1,0:T(8,128)(2,1)}, bf16[256,5248]{1,0:T(8,128)(2,1)}, u32[]{:S(2)}, u32[]{:S(2)}) collective-permute-start(bf16[256,5248]{1,0:T(8,128)(2,1)} %constant_dynamic-slice_fusion.1), channel_id=1, source_target_pairs={{0,1},{1,0},{2,3},{3,2},{4,5},{5,4},{6,7},{7,6},{8,9},{9,8},{10,11... | collective-permute-start | bytes 8060936 | tf_op jit(solution)/shard_map/ppermute | solution.py:236
  83.0 136.3 %collective-permute-start.2 = (bf16[256,1024]{1,0:T(8,128)(2,1)}, bf16[256,1024]{1,0:T(8,128)(2,1)}, u32[]{:S(2)}, u32[]{:S(2)}) collective-permute-start(bf16[256,1024]{1,0:T(8,128)(2,1)} %constant_dynamic-slice_fusion.2), channel_id=1, source_target_pairs={{0,1},{1,0},{2,3},{3,2},{4,5},{5,4},{6,7},{7,6},{8,9},{9,8},{10,11... | collective-permute-start | bytes 1572872 | tf_op jit(solution)/shard_map/ppermute | solution.py:236
  128.5 74.9 %all-to-all-start.2 = ((bf16[16,192,512]{2,1,0:T(8,128)(2,1)}), bf16[16,192,512]{2,1,0:T(8,128)(2,1)}, u32[]{:S(2)}, u32[]{:S(2)}) async-start(bf16[16,192,512]{2,1,0:T(8,128)(2,1)} %pad_maximum_fusion.6), calls=%async_computation.2 | async-start | bytes 6291456 | tf_op jit(solution)/shard_map/all_to_all | solution.py:464
  195.5 95.6 %collective-permute-start.7 = (bf16[656,1024]{1,0:T(8,128)(2,1)}, bf16[656,1024]{1,0:T(8,128)(2,1)}, u32[]{:S(2)}, u32[]{:S(2)}) collective-permute-start(bf16[656,1024]{1,0:T(8,128)(2,1)} %collective-permute-done.6), channel_id=1, source_target_pairs={{0,2},{2,0},{4,6},{6,4},{8,10},{10,8},{12,14},{14,12},{16,18},{18,... | collective-permute-start | bytes 4030472 | tf_op jit(solution)/shard_map/ppermute | solution.py:236
  203.4 94.0 %all-to-all-start.1 = ((bf16[16,64,512]{2,1,0:T(8,128)(2,1)}), bf16[16,64,512]{2,1,0:T(8,128)(2,1)}, u32[]{:S(2)}, u32[]{:S(2)}) async-start(bf16[16,64,512]{2,1,0:T(8,128)(2,1)} %copy-done.6), calls=%async_computation.1 | async-start | bytes 2097152 | tf_op jit(solution)/shard_map/all_to_all | solution.py:467
  218.8 545.1 %all-gather.4.cloned.1.call-start = ((), (), s32[]{:S(2)}) async-start(), calls=%async_computation.8 | async-start | bytes 35651584 | tf_op jit(solution)/shard_map/all_gather | solution.py:513
  218.9 89.2 %collective-permute-start.5 = (bf16[256,5248]{1,0:T(8,128)(2,1)}, bf16[256,5248]{1,0:T(8,128)(2,1)}, u32[]{:S(2)}, u32[]{:S(2)}) collective-permute-start(bf16[256,5248]{1,0:T(8,128)(2,1)} %collective-permute-done.4), channel_id=1, source_target_pairs={{0,2},{2,0},{4,6},{6,4},{8,10},{10,8},{12,14},{14,12},{16,18},{18,... | collective-permute-start | bytes 8060936 | tf_op jit(solution)/shard_map/ppermute | solution.py:236
  219.3 68.6 %collective-permute-start.3 = (bf16[256,1024]{1,0:T(8,128)(2,1)}, bf16[256,1024]{1,0:T(8,128)(2,1)S(1)}, u32[]{:S(2)}, u32[]{:S(2)}) collective-permute-start(bf16[256,1024]{1,0:T(8,128)(2,1)} %collective-permute-done.2), channel_id=1, source_target_pairs={{0,2},{2,0},{4,6},{6,4},{8,10},{10,8},{12,14},{14,12},{16,18},{18,... | collective-permute-start | bytes 1572872 | tf_op jit(solution)/shard_map/ppermute | solution.py:236
  297.3 84.2 %all-to-all-start.3 = ((bf16[16,64,512]{2,1,0:T(8,128)(2,1)}), bf16[16,64,512]{2,1,0:T(8,128)(2,1)}, u32[]{:S(2)}, u32[]{:S(2)}) async-start(bf16[16,64,512]{2,1,0:T(8,128)(2,1)} %get-tuple-element.56), calls=%async_computation.3 | async-start | bytes 2097152 | tf_op jit(solution)/shard_map/all_to_all | solution.py:467
  385.3 100.6 %all-to-all-start.4 = ((bf16[16,64,512]{2,1,0:T(8,128)(2,1)}), bf16[16,64,512]{2,1,0:T(8,128)(2,1)}, u32[]{:S(2)}, u32[]{:S(2)}) async-start(bf16[16,64,512]{2,1,0:T(8,128)(2,1)} %bitcast.198), calls=%async_computation.4 | async-start | bytes 2097152 | tf_op jit(solution)/shard_map/all_to_all | solution.py:464
  525.1 19.4 %collective-permute-start.8 = (bf16[1504,32,128]{2,1,0:T(8,128)(2,1)}, bf16[1504,32,128]{2,1,0:T(8,128)(2,1)}, u32[]{:S(2)}, u32[]{:S(2)}) collective-permute-start(bf16[1504,32,128]{2,1,0:T(8,128)(2,1)} %get-tuple-element.67), channel_id=1, source_target_pairs={{0,2},{2,0},{4,6},{6,4},{8,10},{10,8},{12,14},{14,12},{16,18},{18,... | collective-permute-start | bytes 36962312 | tf_op jit(solution)/shard_map/ppermute | solution.py:236
  538.7 112.9 %all-to-all-start.6 = ((bf16[16,64,512]{2,1,0:T(8,128)(2,1)}), bf16[16,64,512]{2,1,0:T(8,128)(2,1)S(1)}, u32[]{:S(2)}, u32[]{:S(2)}) async-start(bf16[16,64,512]{2,1,0:T(8,128)(2,1)} %bitcast.30), calls=%async_computation.6 | async-start | bytes 2097152 | tf_op jit(solution)/shard_map/all_to_all | solution.py:464
  555.9 84.5 %collective-permute-start.10 = (bf16[376,32,128]{2,1,0:T(8,128)(2,1)}, bf16[376,32,128]{2,1,0:T(8,128)(2,1)}, u32[]{:S(2)}, u32[]{:S(2)}) collective-permute-start(bf16[376,32,128]{2,1,0:T(8,128)(2,1)} %get-tuple-element.162), channel_id=1, source_target_pairs={{0,4},{2,6},{4,0},{6,2},{8,12},{10,14},{12,8},{14,10},{16,20},{18,... | collective-permute-start | bytes 9240584 | tf_op jit(solution)/shard_map/ppermute | solution.py:236
  557.8 82.6 %collective-permute-start.9 = (bf16[376,32,128]{2,1,0:T(8,128)(2,1)}, bf16[376,32,128]{2,1,0:T(8,128)(2,1)}, u32[]{:S(2)}, u32[]{:S(2)}) collective-permute-start(bf16[376,32,128]{2,1,0:T(8,128)(2,1)} %get-tuple-element.163), channel_id=1, source_target_pairs={{0,1},{1,0},{2,3},{3,2},{4,5},{5,4},{6,7},{7,6},{8,9},{9,8},{10,11... | collective-permute-start | bytes 9240584 | tf_op jit(solution)/shard_map/ppermute | solution.py:236
  644.1 119.7 %collective-permute-start.11 = (bf16[188,32,128]{2,1,0:T(8,128)(2,1)}, bf16[188,32,128]{2,1,0:T(8,128)(2,1)}, u32[]{:S(2)}, u32[]{:S(2)}) collective-permute-start(bf16[188,32,128]{2,1,0:T(8,128)(2,1)} %get-tuple-element.180), channel_id=1, source_target_pairs={{0,4},{2,6},{4,0},{6,2},{8,12},{10,14},{12,8},{14,10},{16,20},{18,... | collective-permute-start | bytes 4620296 | tf_op jit(solution)/shard_map/ppermute | solution.py:236
  648.1 115.8 %collective-permute-start.12 = (bf16[188,32,128]{2,1,0:T(8,128)(2,1)}, bf16[188,32,128]{2,1,0:T(8,128)(2,1)}, u32[]{:S(2)}, u32[]{:S(2)}) collective-permute-start(bf16[188,32,128]{2,1,0:T(8,128)(2,1)} %get-tuple-element.178), channel_id=1, source_target_pairs={{0,1},{1,0},{2,3},{3,2},{4,5},{5,4},{6,7},{7,6},{8,9},{9,8},{10,11... | collective-permute-start | bytes 4620296 | tf_op jit(solution)/shard_map/ppermute | solution.py:236
  652.5 130.2 %all-to-all-start.5 = ((bf16[16,192,512]{2,1,0:T(8,128)(2,1)}), bf16[16,192,512]{2,1,0:T(8,128)(2,1)S(1)}, u32[]{:S(2)}, u32[]{:S(2)}) async-start(bf16[16,192,512]{2,1,0:T(8,128)(2,1)} %get-tuple-element.72), calls=%async_computation.5 | async-start | bytes 6291456 | tf_op jit(solution)/shard_map/all_to_all | solution.py:467
  782.7 11.8 %collective-permute-start.13 = (bf16[192,1024]{1,0:T(8,128)(2,1)}, bf16[192,1024]{1,0:T(8,128)(2,1)}, u32[]{:S(2)}, u32[]{:S(2)}) collective-permute-start(bf16[192,1024]{1,0:T(8,128)(2,1)} %fusion.74), channel_id=1, source_target_pairs={{0,1},{1,0},{2,3},{3,2},{4,5},{5,4},{6,7},{7,6},{8,9},{9,8},{10,11... | collective-permute-start | bytes 1179656 | tf_op jit(solution)/shard_map/ppermute | solution.py:236
  782.7 134.4 %all-to-all-start.7 = ((bf16[16,192,512]{2,1,0:T(8,128)(2,1)}), bf16[16,192,512]{2,1,0:T(8,128)(2,1)}, u32[]{:S(2)}, u32[]{:S(2)}) async-start(bf16[16,192,512]{2,1,0:T(8,128)(2,1)} %get-tuple-element.79), calls=%async_computation.7 | async-start | bytes 6291456 | tf_op jit(solution)/shard_map/all_to_all | solution.py:467
  788.8 179.2 %all-gather.6.cloned.1.call-start = ((), (), s32[]{:S(2)}) async-start(), calls=%async_computation.9 | async-start | bytes 6684672 | tf_op jit(solution)/shard_map/all_gather | solution.py:617
  825.2 88.2 %collective-permute-start.14 = (bf16[2,94,32,128]{3,2,1,0:T(8,128)(2,1)S(1)}, bf16[2,94,32,128]{3,2,1,0:T(8,128)(2,1)S(1)}, u32[]{:S(2)}, u32[]{:S(2)}) collective-permute-start(bf16[2,94,32,128]{3,2,1,0:T(8,128)(2,1)S(1)} %pad_maximum_fusion.12), channel_id=1, source_target_pairs={{0,8},{2,10},{4,12},{6,14},{8,0},{10,2},{12,4},{14,6},{16,24},{18,... | collective-permute-start | bytes 4620296 | tf_op jit(solution)/shard_map/ppermute | solution.py:236
  914.5 36.1 %collective-permute-start.15 = (bf16[94,32,128]{2,1,0:T(8,128)(2,1)S(1)}, bf16[94,32,128]{2,1,0:T(8,128)(2,1)S(1)}, u32[]{:S(2)}, u32[]{:S(2)}) collective-permute-start(bf16[94,32,128]{2,1,0:T(8,128)(2,1)S(1)} %fusion.98), channel_id=1, source_target_pairs={{0,16},{2,18},{4,20},{6,22},{8,24},{10,26},{12,28},{14,30},{16,0},... | collective-permute-start | bytes 2310152 | tf_op jit(solution)/shard_map/ppermute | solution.py:236
  931.3 20.4 %collective-permute-start.16 = (f32[2,1024]{1,0:T(2,128)S(1)}, f32[2,1024]{1,0:T(2,128)S(1)}, u32[]{:S(2)}, u32[]{:S(2)}) collective-permute-start(f32[2,1024]{1,0:T(2,128)S(1)} %pad_maximum_fusion.15), channel_id=1, source_target_pairs={{0,2},{2,0},{4,6},{6,4},{8,10},{10,8},{12,14},{14,12},{16,18},{18,... | collective-permute-start | bytes 24584 | tf_op jit(solution)/shard_map/ppermute | solution.py:236
  951.7 3.7 collective-permute-start.17
  955.4 3.7 collective-permute-start.18
  959.2 4.6 collective-permute-start.19
  963.8 3.7 collective-permute-start.20
  (104 other events, 1789.4 us)
Sparse Core Ops, SparseCore 0:
  221.8 210.1 all-gather.3
  796.7 104.0 all-gather.5
where the time goes:
time: 1040 us; the launch traced here: 1030 us
  Pallas kernels  371 us (36%)
  matrix products  160 us (15%)
  waiting for transfers between devices  151 us (15%)
  other arithmetic  120 us (12%)
  starting transfers between devices  90.8 us (9%)
  local copies, waits for them, and re-layouts  82.8 us (8%)
  blocking collectives  33.9 us (3%)
  between operations  16.1 us (2%)
    pallas_call x2, Pallas kernels, attend_backward(): pl.pallas_call(functools.partial(bwd_kernel, bq, bk, sub), out_shape=(jax...  188 us
    dot_general x21, matrix products, mm(): lax.dot_general(a, b, (((da,), (db,)), ((), ())), preferred_element_type=...  160 us
    pallas_call x2, Pallas kernels, attend_forward(): pl.pallas_call(functools.partial(fwd_kernel, bq, bk, sub), out_shape=(jax...  117 us
    ppermute x21, waiting for transfers between devices, swap_bit(): return lax.ppermute(x, axis, [(s, s ^ bit) for s in range(n)])  109 us
    unnamed x220, local copies, waits for them, and re-layouts  64.5 us
    all_to_all x4, waiting for transfers between devices, spread(): return lax.all_to_all(x, 'ctx', 0, 0, tiled=True)  42.3 us
    pallas_call x1, Pallas kernels, scatter_tiles(): pl.pallas_call(functools.partial(scatter_kernel, counts, parts), out_shap...  39 us
    all_to_all x4, starting transfers between devices, spread(): return lax.all_to_all(x, 'ctx', 0, 0, tiled=True)  34 us
  transfers between devices with their start and end apart: 31, of which 10 were waited for; matrix products, arithmetic and copies ran while one was open for 30% of the time, Pallas kernels for 33%

commit v1 on v0

--- a/solution.py
+++ b/solution.py
@@ -331,7 +331,7 @@
     )(where, *grads)
 
 
-def soap_kernel(block, kind_ref, row_ref, col_ref, odd_ref, live_ref, qkv, early, master, first, second, left, right,
+def soap_kernel(block, kind_ref, pick_ref, live_ref, pool, early, master, first, second, left, right,
                 grads_out, master_out, copy_out, first_out, second_out, tiles, sem):
     step = pl.program_id(0)
     total = tiles.shape[0]
@@ -339,10 +339,7 @@
     @pl.when(step == 0)
     def _():
         def fetch(n, carry):
-            rows = pl.ds(pl.multiple_of(row_ref[n], 64), 64)
-            cols = pl.ds(pl.multiple_of(col_ref[n], 128), 128)
-
-            pltpu.make_async_copy(qkv.at[rows, cols], tiles.at[n], sem).start()
+            pltpu.make_async_copy(pool.at[pick_ref[n]], tiles.at[n], sem).start()
             return carry
 
         lax.fori_loop(0, total, fetch, 0)
@@ -367,10 +364,8 @@
 
         def own_tile(k):
             n = jnp.minimum(step * block + k, total - 1)
-            pair = tiles[n].astype(F32)
-            turned = jnp.where(odd_ref[n] == 1, pair[:, 64:128], pair[:, 0:64]).T
-            flat = early[k].astype(F32)
-            tile = jnp.where(kind_ref[n] != 0, turned, jnp.concatenate([flat[:, 0:64], flat[:, 64:128]], axis=0))
+            flat = jnp.where(kind_ref[n] != 0, tiles[n].astype(F32), early[k].astype(F32))
+            tile = jnp.concatenate([flat[:, 0:64], flat[:, 64:128]], axis=0)
             return jnp.where(live_ref[n] != 0, tile, 0.0)
 
         lives = [live_ref[jnp.minimum(step * block + k, total - 1)] != 0 for k in group]
@@ -392,7 +387,7 @@
             second_out[k] = jnp.where(live, s, second[k])
 
 
-def soap_step(picks, qkv, early, master, first, second, left, right):
+def soap_step(picks, pool, early, master, first, second, left, right):
     cap = master.shape[0]
     block = min(16, cap)
     spec = pl.BlockSpec((block, 64, 64), lambda i: (i, 0, 0))
@@ -402,27 +397,84 @@
         functools.partial(soap_kernel, block),
         grid=(-(-cap // block),),
         out_shape=(like, like, jax.ShapeDtypeStruct(master.shape, BF), like, like),
-        in_specs=[SM] * 5 + [whole, pl.BlockSpec((block, 32, 128), lambda i: (i, 0, 0))] + [spec] * 5,
+        in_specs=[SM] * 3 + [whole, pl.BlockSpec((block, 32, 128), lambda i: (i, 0, 0))] + [spec] * 5,
         out_specs=(spec,) * 5,
-        scratch_shapes=[pltpu.VMEM((cap, 64, 128), BF), pltpu.SemaphoreType.DMA],
+        scratch_shapes=[pltpu.VMEM((cap, 32, 128), BF), pltpu.SemaphoreType.DMA],
         compiler_params=pltpu.CompilerParams(vmem_limit_bytes=40 << 20),
-        cost_estimate=pl.CostEstimate(flops=1 << 30, bytes_accessed=30 << 20, transcendentals=0),
+        cost_estimate=pl.CostEstimate(flops=23 << 30, bytes_accessed=30 << 20, transcendentals=0),
         name="soap",
-    )(*picks, qkv, early, master, first, second, left, right)
-
-
-def own_picks(slot_table, slot_cap, heads):
+    )(*picks, pool, early, master, first, second, left, right)
+
+
+def own_tiles(slot_table, slot_cap):
     device_index = lax.axis_index(("ctx", "fsdp"))
     own_ids = device_index * slot_cap + jnp.arange(slot_cap, dtype=jnp.int32)
     hit = slot_table[None, :] == own_ids[:, None]
     live = jnp.any(hit, axis=1).astype(jnp.int32)
     tile = jnp.sum(jnp.where(hit, jnp.arange(slot_table.shape[0], dtype=jnp.int32)[None, :], 0), axis=1)
-    across = heads * HEAD // 64
-    is_qkv = tile < 3 * across * across
-    q_row, q_col = tile // (3 * across), tile % (3 * across)
-    row = jnp.where(is_qkv, (q_col % across) * 3 + q_col // across, 0)
-    col = jnp.where(is_qkv, q_row, 0)
-    return is_qkv.astype(jnp.int32), row * 64, (col // 2) * 128, col % 2, live
+    return tile, live
+
+
+ROUND = 8
+
+
+def all_tiles(gathered):
+    heads, _, width = gathered.shape
+    tiles = gathered.reshape(heads, 3, HEAD, width // 64, 2, 32).transpose(3, 1, 0, 5, 4, 2)
+    return tiles.reshape(-1, 32, 128)
+
+
+def pack_kernel(place_ref, grad, out):
+    lane = lax.broadcasted_iota(jnp.int32, (32, 128), 1) < 64
+    rows, width = grad.shape
+    for part in range(rows // 64):
+        for pair in range(width // 128):
+            both = grad[part * 64 : part * 64 + 64, pair * 128 : pair * 128 + 128].astype(F32).T
+            for odd in range(2):
+                tile = both[odd * 64 : odd * 64 + 64]
+                wide = jnp.concatenate([tile[0:32], tile[32:64]], axis=1)
+                out[place_ref[part * (width // 64) + pair * 2 + odd]] = wide.astype(BF)
+
+
+def pack_tiles(place, grad, count):
+    return pl.pallas_call(
+        pack_kernel,
+        out_shape=jax.ShapeDtypeStruct((count + 1, 32, 128), BF),
+        in_specs=[SM, VM],
+        out_specs=VM,
+        compiler_params=pltpu.CompilerParams(vmem_limit_bytes=16 << 20),
+        cost_estimate=pl.CostEstimate(flops=1 << 30, bytes_accessed=2 << 20, transcendentals=0),
+        name="pack_tiles",
+    )(place, grad)
+
+
+def send_tiles(slot_table, slot_cap, grad, own):
+    ctx_size, fsdp_size = lax.axis_size("ctx"), lax.axis_size("fsdp")
+    ctx_index, fsdp_index = lax.axis_index("ctx"), lax.axis_index("fsdp")
+    across = grad.shape[1] // 64
+    heads, per = ctx_size, 3 * across
+    owner = (slot_table[: 3 * across * heads] // slot_cap).reshape(across, 3, heads).transpose(2, 1, 0).reshape(heads, per)
+    earlier = jnp.arange(per)[:, None] > jnp.arange(per)[None, :]
+    rank = jnp.sum(((owner[:, :, None] == owner[:, None, :]) & earlier[None]).astype(jnp.int32), axis=2)
+    mine, my_rank = owner[ctx_index], rank[ctx_index]
+    to_us = mine % fsdp_size == fsdp_index
+
+    here = to_us & (my_rank < ROUND)
+    place = jnp.where(here, (mine // fsdp_size) * ROUND + my_rank, ctx_size * ROUND)
+    packed = pack_tiles(place, grad, ctx_size * ROUND)[: ctx_size * ROUND]
+    got = lax.all_to_all(packed.reshape(ctx_size, ROUND, 32, 128), "ctx", 0, 0, tiled=True)
+
+    def whole(grad):
+        return all_tiles(lax.all_gather(grad[None], "ctx", axis=0, tiled=True))
+
+    rest = lax.cond(
+        jnp.max(rank) >= ROUND, whole, lambda grad: jnp.zeros((heads * per, 32, 128), BF), after(grad, got)
+    )
+    row, part, head = own // (3 * heads), (own // heads) % 3, own % heads
+    own_rank = rank.reshape(-1)[jnp.clip(head * per + part * across + row, 0, heads * per - 1)]
+    early = own_rank < ROUND
+    place = jnp.where(early, head * ROUND + own_rank, ctx_size * ROUND + own)
+    return jnp.concatenate([got.reshape(-1, 32, 128), rest], axis=0), place, got
 
 
 def gain_step(grads_in, gains_old, first_old, second_old):
@@ -517,7 +569,7 @@
         twins = [after(swap_bit(g, "ctx", 1), outs[-1]) for g in got_later]
         full_out, full_in, full_down = (joined(*parts) for parts in zip(later, got_later, twins))
 
-    outputs_list, d_middles, d_att_all = [], [], []
+    results, d_middles, d_att_all = [], [], []
     hidden_all, d_gate_all, normed_two_all, branch_all = [], [], [], []
     gain_two_sum = 0.0
     for b in range(micro):
@@ -530,8 +582,7 @@
         d_hidden = mm(grad_top, full_down, 1, 1)
         hidden, d_gate_up = gated_both(gate_up, d_hidden)
         hidden, d_gate_up = hidden.astype(BF), d_gate_up.astype(BF)
-        result = middle_value + mm(hidden, full_down, 1, 0)
-        outputs_list.append(result.astype(BF))
+        results.append((middle_value, hidden))
         d_normed_two = mm(d_gate_up, full_in, 1, 1)
         d_mid_norm, gain_two = norm_back(middle_value, gains[1], d_normed_two)
         d_middle = grad_top.astype(F32) + d_mid_norm
@@ -603,32 +654,44 @@
             next_near = [after(v, grads) for v in next_near]
             pair = [(t.reshape(2, 2, -1, 32, 128), v.reshape(2, 2, -1, 32, 128)) for t, v in zip(next_ours, next_near)]
             kept, sent = (jnp.concatenate([t[side] + v[side] for t, v in pair], axis=1) for side in (0, 1))
+            flat = after(flat, sent)
             got = swap_bit(sent, "ctx", 4)
             kept, sent = (kept[side] + got[side] for side in (0, 1))
+            first_turn = got
             own_slots = kept + swap_bit(sent, "ctx", 8)
-        d_proj_all.append(collect(grads))
+        last_grads = grads
+        if b + 1 < micro:
+            d_proj_all.append(collect(grads))
         grad_heads = grad_heads + mm(flat, normed_wide[b], 1, 0)
 
+    states = [master, first_moment, rotated_second_moments, row_eigenbasis, column_eigenbasis]
+    outputs_list = [(m + mm(h, full_down, 1, 0)).astype(BF) for m, h in results]
+    own, live = own_tiles(slot_table, slot_cap)
+    is_qkv = own < 3 * heads * (width // 64)
+    share = lax.dynamic_index_in_dim(full_qkv.reshape(width, 3, heads, HEAD), ctx_index // copies, 2, keepdims=False)
+    gain_one = jnp.sum(grad_heads * share.reshape(width, 3 * HEAD).T.astype(F32), axis=0) / (gains[0] * copies)
     grad_heads = after(grad_heads.astype(BF), d_proj_all[0], *(next_near if fast else ()))
-    if lax.axis_size("fsdp") == 2:
-        grad_heads = grad_heads + swap_bit(grad_heads, "fsdp", 1)
+    if fast and heads == ctx_size:
+        grad_heads = after(grad_heads + swap_bit(grad_heads, "fsdp", 1), first_turn)
+        pool, place, first_round = send_tiles(slot_table, slot_cap, grad_heads, own)
+        last_grads = after(last_grads, first_round, own_slots, pool, *outputs_list)
     else:
         grad_heads = lax.psum(grad_heads, "fsdp")
-    grad_qkv = lax.all_gather(grad_heads[None], "ctx", axis=0, tiled=True)[::copies].reshape(3 * width, width)
+        pool = all_tiles(lax.all_gather(grad_heads[None], "ctx", axis=0, tiled=True)[::copies])
+        place = own
+    d_proj_all.append(collect(last_grads))
+    picks = (is_qkv.astype(jnp.int32), jnp.where(is_qkv, place, 0), live)
 
     input_grads = []
-    gain_one_sum = 0.0
     for b in range(micro):
         d_proj = d_proj_all[b].reshape(heads, 3, HEAD, shard).transpose(1, 0, 2, 3).reshape(3 * width, shard)
         d_normed = mm(d_proj, full_qkv, 0, 1)
-        d_in_norm, gain_one = norm_back(layer_ins[b], gains[0], d_normed)
+        d_in_norm, _ = norm_back(layer_ins[b], gains[0], d_normed)
         input_grads.append((d_middles[b] + d_in_norm).astype(BF))
-        gain_one_sum = gain_one_sum + gain_one
-    gain_grads = sum_all(jnp.stack([gain_one_sum, gain_two_sum]))
-
-    picks = own_picks(slot_table, slot_cap, heads)
+    gain_grads = sum_all(after(jnp.stack([gain_one, gain_two_sum]), d_proj_all[-1]))
+
     own_grads, new_master, new_copy, new_first, new_second = soap_step(
-        picks, grad_qkv, own_slots, master, first_moment, rotated_second_moments, row_eigenbasis, column_eigenbasis
+        picks, pool, own_slots, *states
     )
     new_gains, new_gain_first, new_gain_second = gain_step(gain_grads, gain_master, gain_first, gain_second)
     return (

time: 1040 us -> 1020 us (0.981)
  waiting for transfers between devices: 151 us -> 90.3 us
  starting transfers between devices: 90.8 us -> 123 us
  Pallas kernels: 371 us -> 345 us
  other arithmetic: 120 us -> 137 us
    ppermute x21, waiting for transfers between devices: 109 us -> 55.3 us  [swap_bit(): return lax.ppermute(x, axis, [(s, s ^ bit) for s in range(n)])]
    ppermute x21, starting transfers between devices: 22.8 us -> 55 us  [swap_bit(): return lax.ppermute(x, axis, [(s, s ^ bit) for s in range(n)])]
    pallas_call x2, Pallas kernels: 188 us -> 177 us  [attend_backward(): pl.pallas_call(functools.partial(bwd_kernel, bq, bk, sub), out_shape=(jax...]
    unnamed x220 -> x233, local copies, waits for them, and re-layouts: 64.5 us -> 63.8 us
  transfers between devices with their start and end apart: 31 -> 31, of which waited for: 10 -> 7; matrix products, arithmetic and copies ran while one was open for 30% -> 34% of each run, Pallas kernels for 33% -> 34%
where the time goes in v1:
time: 1020 us; the launch traced here: 1000 us
  Pallas kernels  345 us (34%)
  matrix products  165 us (16%)
  other arithmetic  137 us (13%)
  starting transfers between devices  123 us (12%)
  waiting for transfers between devices  90.3 us (9%)
  local copies, waits for them, and re-layouts  90.1 us (9%)
  blocking collectives  33.9 us (3%)
  between operations  16.5 us (2%)
    pallas_call x2, Pallas kernels, attend_backward(): pl.pallas_call(functools.partial(bwd_kernel, bq, bk, sub), out_shape=(jax...  177 us
    dot_general x21, matrix products, mm(): lax.dot_general(a, b, (((da,), (db,)), ((), ())), preferred_element_type=...  165 us
    pallas_call x2, Pallas kernels, attend_forward(): pl.pallas_call(functools.partial(fwd_kernel, bq, bk, sub), out_shape=(jax...  108 us
    unnamed x233, local copies, waits for them, and re-layouts  63.8 us
    ppermute x21, waiting for transfers between devices, swap_bit(): return lax.ppermute(x, axis, [(s, s ^ bit) for s in range(n)])  55.3 us
    ppermute x21, starting transfers between devices, swap_bit(): return lax.ppermute(x, axis, [(s, s ^ bit) for s in range(n)])  55 us
    pallas_call x1, Pallas kernels, scatter_tiles(): pl.pallas_call(functools.partial(scatter_kernel, counts, parts), out_shap...  39 us
    all_to_all x4, waiting for transfers between devices, spread(): return lax.all_to_all(x, 'ctx', 0, 0, tiled=True)  34.9 us
  transfers between devices with their start and end apart: 31, of which 7 were waited for; matrix products, arithmetic and copies ran while one was open for 34% of the time, Pallas kernels for 34%

profile of v1, /device:TPU:0, one launch (start us, length us, event | category | flops | bytes accessed | tf_op | source)
XLA Modules:
  0.0 1001.0 jit_solution(8036888930043030082)
XLA Ops:
  18.4 33.9 %all_gather.9 = bf16[2,1024]{1,0:T(2,128)(2,1)S(1)} all-gather(bf16[2,512]{1,0:T(2,128)(2,1)S(1)} %copy-done.108), channel_id=1, replica_groups=mesh['ctx'=16,'fsdp'=2] {'fsdp'}, dimensions={1}, use_global_device_ids=true | all-gather | bytes 6144 | tf_op jit(solution)/shard_map/all_gather | solution.py:522
  66.8 6.8 all-to-all-start
  98.1 34.8 %all-to-all-done.qkv_ref = bf16[16,192,512]{2,1,0:T(8,128)(2,1)S(1)} async-done(((bf16[16,192,512]{2,1,0:T(8,128)(2,1)}), bf16[16,192,512]{2,1,0:T(8,128)(2,1)S(1)}, u32[]{:S(2)}, u32[]{:S(2)}) %all-to-all-start) | async-done | bytes 3145760 | tf_op jit(solution)/shard_map/all_to_all | solution.py:516
  132.9 15.5 %all-to-all-start.2 = ((bf16[16,192,512]{2,1,0:T(8,128)(2,1)}), bf16[16,192,512]{2,1,0:T(8,128)(2,1)}, u32[]{:S(2)}, u32[]{:S(2)}) async-start(bf16[16,192,512]{2,1,0:T(8,128)(2,1)} %pad_maximum_fusion.7), calls=%async_computation.2 | async-start | bytes 6291456 | tf_op jit(solution)/shard_map/all_to_all | solution.py:516
  148.4 59.9 %attend_fwd.2 = (bf16[16,64,512]{2,1,0:T(8,128)(2,1)S(1)}, f32[64,8192]{1,0:T(8,128)S(1)}, f32[1,8192]{1,0:T(1,128)S(1)}) custom-call(s32[8]{0:T(128)S(1)} %get-tuple-element.276.lo_ref, s32[8]{0:T(128)S(1)} %get-tuple-element.278.hi_ref, bf16[16,192,512]{2,1,0:T(8,128)(2,1)S(1)} %all-to-all-done.qkv_ref, s32[1,8192]{1,0:T(1,128)S(1)} %get-tuple-element.246.seg_ref), custom_call_target="tpu_custom_call" | custom-call | flops 76504104960 | bytes 8388608 | tf_op jit(solution)/shard_map/attend_fwd/pallas_call | solution.py:157
  211.6 11.7 %all-to-all-start.1 = ((bf16[16,64,512]{2,1,0:T(8,128)(2,1)}), bf16[16,64,512]{2,1,0:T(8,128)(2,1)}, u32[]{:S(2)}, u32[]{:S(2)}) async-start(bf16[16,64,512]{2,1,0:T(8,128)(2,1)} %copy-done.5), calls=%async_computation.1 | async-start | bytes 2097152 | tf_op jit(solution)/shard_map/all_to_all | solution.py:519
  224.1 48.5 %attend_fwd.3 = (bf16[16,64,512]{2,1,0:T(8,128)(2,1)}, f32[64,8192]{1,0:T(8,128)S(1)}, f32[1,8192]{1,0:T(1,128)S(1)}) custom-call(s32[8]{0:T(128)S(1)} %get-tuple-element.275.lo_ref, s32[8]{0:T(128)S(1)} %get-tuple-element.277.hi_ref, bf16[16,192,512]{2,1,0:T(8,128)(2,1)} %all-to-all-done.2.qkv_ref, s32[1,8192]{1,0:T(1,128)S(1)} %get-tuple-element.247.seg_ref), custom_call_target="tpu_custom_call" | custom-call | flops 76504104960 | bytes 8388608 | tf_op jit(solution)/shard_map/attend_fwd/pallas_call | solution.py:157
  303.7 8.3 fusion.139
  312.0 13.5 %multiply_convert_fusion.1 = (bf16[512,2624]{1,0:T(8,128)(2,1)}, f32[512,2624]{1,0:T(8,128)S(1)}) fusion(f32[512,5248]{1,0:T(8,128)S(1)} %fusion.139), kind=kLoop, calls=%fused_computation.41 | loop fusion | flops 88670208 | bytes 18808832 | tf_op jit(solution)/shard_map/convert_element_type | solution.py:584
  325.4 12.9 %bitcast_multiply_fusion.3 = (f32[512,2624]{1,0:T(8,128)}, f32[512,2624]{1,0:T(8,128)}) fusion(f32[512,2624]{1,0:T(8,128)S(1)} %get-tuple-element.189, f32[512,5248]{1,0:T(8,128)} %copy-done.36, bf16[2,512,1024]{2,1,0:T(8,128)(2,1)S(1)} %copy-done.37, bf16[1312,1024]{1,0:T(8,128)(2,1)} %get-tuple-element.213, bf16[1312,1024]{1,0:T(8,128)(2,1)} %get-tuple-element.212), kind=kOutput, calls=%fused_computation.25 | convolution fusion | flops 2783707136 | bytes 33423360 | tf_op jit(solution)/shard_map/dot_general | solution.py:227
  338.4 8.4 add_convert_fusion.1
  346.7 14.6 %multiply_reduce_fusion.1 = (f32[1024]{0:T(1024)}, f32[512]{0:T(512)S(1)}, f32[512,1024]{1,0:T(8,128)}) fusion(f32[512,1024]{1,0:T(8,128)} %copy-done.19, f32[512]{0:T(512)S(1)} %fusion.117, f32[512]{0:T(512)S(1)} %broadcast_multiply_fusion.1, f32[1024]{0:T(1024)S(1)} %bitcast.246, bf16[512,5248]{1,0:T(8,128)(2,1)} %add_convert_fusion.1, ...), kind=kOutput, calls=%fused_computation.135 | convolution fusion | flops 5528091136 | bytes 20330496 | tf_op jit(solution)/shard_map/dot_general | solution.py:227
  382.4 9.2 fusion.137
  391.6 18.2 %bitcast_multiply_fusion.1 = (f32[512,2624]{1,0:T(8,128)}, f32[512,2624]{1,0:T(8,128)S(1)}, f32[2624,512]{0,1:T(8,128)}) fusion(f32[512,5248]{1,0:T(8,128)S(1)} %fusion.137, bf16[2,512,1024]{2,1,0:T(8,128)(2,1)S(1)} %copy-done.39, bf16[1312,1024]{1,0:T(8,128)(2,1)} %get-tuple-element.213, bf16[1312,1024]{1,0:T(8,128)(2,1)S(1)} %copy-done.53), kind=kOutput, calls=%fused_computation.23 | convolution fusion | flops 2849538048 | bytes 28049408 | tf_op jit(solution)/shard_map/dot_general | solution.py:227
  409.9 7.1 multiply_add_fusion
  417.0 8.3 add_convert_fusion
  425.3 11.7 %multiply_reduce_fusion = (f32[1024]{0:T(1024)}, f32[512]{0:T(512)S(1)}, f32[512,1024]{1,0:T(8,128)S(1)}) fusion(f32[512,1024]{1,0:T(8,128)S(1)} %copy-done.23, f32[512]{0:T(512)S(1)} %fusion.118, f32[512]{0:T(512)S(1)} %broadcast_multiply_fusion, f32[1024]{0:T(1024)S(1)} %bitcast.249, bf16[512,5248]{1,0:T(8,128)(2,1)} %add_convert_fusion, ...), kind=kOutput, calls=%fused_computation.134 | convolution fusion | flops 5528091136 | bytes 20330496 | tf_op jit(solution)/shard_map/dot_general | solution.py:227
  440.2 18.8 %convolution_convert_fusion.refs_1_ = bf16[1024,5248]{1,0:T(8,128)(2,1)} fusion(bf16[512,5248]{1,0:T(8,128)(2,1)} %add_convert_fusion, bf16[512,5248]{1,0:T(8,128)(2,1)} %add_convert_fusion.1, bf16[512,1024]{1,0:T(8,128)(2,1)S(1)} %copy-done.67, bf16[512,1024]{1,0:T(8,128)(2,1)S(1)} %copy-done.65), kind=kOutput, calls=%fused_computation.5 | convolution fusion | flops 11036917760 | bytes 23592960 | tf_op jit(solution)/shard_map/dot_general | solution.py:227
  463.5 7.8 convolution_convert_fusion.1.refs_2_
  471.4 39.0 %scatter_tiles.1 = (bf16[1504,32,128]{2,1,0:T(8,128)(2,1)}, bf16[1504,32,128]{2,1,0:T(8,128)(2,1)}) custom-call(s32[2224]{0:T(1024)S(1)} %select_add_fusion.where_ref, bf16[1024,1024]{1,0:T(8,128)(2,1)S(1)} %fusion.60.refs_0_, bf16[1024,5248]{1,0:T(8,128)(2,1)} %convolution_convert_fusion.refs_1_, bf16[2624,1024]{1,0:T(8,128)(2,1)} %convolution_convert_fusion.1.refs_2_), custom_call_target="tpu_custom_call" | custom-call | flops 42949672960 | bytes 41943040 | tf_op jit(solution)/shard_map/scatter_tiles/pallas_call | solution.py:322
  519.0 8.9 multiply_sine_fusion
  536.2 11.4 %slice_add_fusion = (bf16[376,32,128]{2,1,0:T(8,128)(2,1)}, bf16[376,32,128]{2,1,0:T(8,128)(2,1)}, bf16[376,32,128]{2,1,0:T(8,128)(2,1)S(1)}, bf16[376,32,128]{2,1,0:T(8,128)(2,1)S(1)}) fusion(bf16[1504,32,128]{2,1,0:T(8,128)(2,1)} %collective-permute-done.8, bf16[1504,32,128]{2,1,0:T(8,128)(2,1)} %get-tuple-element.75), kind=kLoop, calls=%fused_computation.79 | loop fusion | flops 6160384 | bytes 36962304 | tf_op jit(solution)/shard_map/add | solution.py:630
  549.5 13.1 %collective-permute-start.9 = (bf16[376,32,128]{2,1,0:T(8,128)(2,1)}, bf16[376,32,128]{2,1,0:T(8,128)(2,1)}, u32[]{:S(2)}, u32[]{:S(2)}) collective-permute-start(bf16[376,32,128]{2,1,0:T(8,128)(2,1)} %get-tuple-element.193), channel_id=1, source_target_pairs={{0,1},{1,0},{2,3},{3,2},{4,5},{5,4},{6,7},{7,6},{8,9},{9,8},{10,11... | collective-permute-start | bytes 9240584 | tf_op jit(solution)/shard_map/ppermute | solution.py:236
  562.6 96.7 %attend_bwd.2 = (bf16[16,192,512]{2,1,0:T(8,128)(2,1)}, bf16[192,8192]{1,0:T(8,128)(2,1)}) custom-call(s32[16]{0:T(128)} %get-tuple-element.273.lo_ref, s32[16]{0:T(128)} %get-tuple-element.274.hi_ref, bf16[16,192,512]{2,1,0:T(8,128)(2,1)} %copy-done, s32[1,8192]{1,0:T(1,128)} %copy-done.7, bf16[16,64,512]{2,1,0:T(8,128)(2,1)} %all-to-all-done.4.do_ref, ...), custom_call_target="tpu_custom_call" | custom-call | flops 106032005120 | bytes 16777216 | tf_op jit(solution)/shard_map/attend_bwd/pallas_call | solution.py:167
  674.3 79.9 %attend_bwd.3 = (bf16[16,192,512]{2,1,0:T(8,128)(2,1)}, bf16[192,8192]{1,0:T(8,128)(2,1)}) custom-call(s32[16]{0:T(128)} %get-tuple-element.271.lo_ref, s32[16]{0:T(128)} %get-tuple-element.272.hi_ref, bf16[16,192,512]{2,1,0:T(8,128)(2,1)} %all-to-all-done.2.qkv_ref, s32[1,8192]{1,0:T(1,128)} %copy-done.6, bf16[16,64,512]{2,1,0:T(8,128)(2,1)} %copy-done.68, ...), custom_call_target="tpu_custom_call" | custom-call | flops 106032005120 | bytes 16777216 | tf_op jit(solution)/shard_map/attend_bwd/pallas_call | solution.py:167
  762.4 8.6 fusion
  771.0 10.1 %fusion.88 = (f32[1024]{0:T(1024)S(1)}, bf16[192,1024]{1,0:T(8,128)(2,1)}) fusion(bf16[1024,3,1,64]{0,3,2,1:T(8,128)(2,1)S(1)} %copy-done.69, f32[192,1024]{1,0:T(8,128)S(1)} %fusion, bf16[192,8192]{1,0:T(8,128)(2,1)S(1)} %copy-done.109, bf16[2,8192,1024]{2,1,0:T(8,128)(2,1)} %all-gather.6.cloned.1.call-done), kind=kOutput, calls=%fused_computation.201 | convolution fusion | flops 3222207488 | bytes 21499904 | tf_op jit(solution)/shard_map/dot_general | solution.py:227
  781.1 14.7 %collective-permute-start.13 = (bf16[192,1024]{1,0:T(8,128)(2,1)}, bf16[192,1024]{1,0:T(8,128)(2,1)}, u32[]{:S(2)}, u32[]{:S(2)}) collective-permute-start(bf16[192,1024]{1,0:T(8,128)(2,1)} %get-tuple-element.95), channel_id=1, source_target_pairs={{0,1},{1,0},{2,3},{3,2},{4,5},{5,4},{6,7},{7,6},{8,9},{9,8},{10,11... | collective-permute-start | bytes 1179656 | tf_op jit(solution)/shard_map/ppermute | solution.py:236
  798.7 6.7 collective-permute-done.13
  817.7 7.5 add_convert_fusion.5
  829.3 43.5 %collective-permute-done.15 = bf16[94,32,128]{2,1,0:T(8,128)(2,1)S(1)} collective-permute-done((bf16[94,32,128]{2,1,0:T(8,128)(2,1)S(1)}, bf16[94,32,128]{2,1,0:T(8,128)(2,1)S(1)}, u32[]{:S(2)}, u32[]{:S(2)}) %collective-permute-start.15) | collective-permute-done | bytes 770080 | tf_op jit(solution)/shard_map/ppermute | solution.py:236
  917.5 20.1 %soap.1 = (f32[94,64,64]{2,1,0:T(8,128)S(1)}, f32[94,64,64]{2,1,0:T(8,128)S(1)}, bf16[94,64,64]{2,1,0:T(8,128)(2,1)S(1)}, f32[94,64,64]{2,1,0:T(8,128)S(1)}, f32[94,64,64]{2,1,0:T(8,128)}) custom-call(s32[94]{0:T(128)S(1)} %compare_convert_fusion.kind_ref, s32[94]{0:T(128)S(1)} %compare_select_fusion.35.pick_ref, s32[94]{0:T(128)S(1)} %convert_element_type.218.live_ref, ...), custom_call_target="tpu_custom_call" | custom-call | flops 24696061952 | bytes 31457280 | tf_op jit(solution)/shard_map/soap/pallas_call | solution.py:396
  (434 shorter events, 277.9 us)
Async XLA Ops:
  14.7 38.1 %collective-permute-start = (bf16[256,3072]{0,1:T(8,128)(2,1)}, bf16[256,3072]{0,1:T(8,128)(2,1)}, u32[]{:S(2)}, u32[]{:S(2)}) collective-permute-start(bf16[256,3072]{0,1:T(8,128)(2,1)} %constant_dynamic-slice_fusion.6), channel_id=1, source_target_pairs={{0,1},{1,0},{2,3},{3,2},{4,5},{5,4},{6,7},{7,6},{8,9},{9,8},{10,11... | collective-permute-start | bytes 4718600 | tf_op jit(solution)/shard_map/ppermute | solution.py:236
  17.7 495.3 %copy-start.6 = (s32[1,8192]{1,0:T(1,128)}, s32[1,8192]{1,0:T(1,128)S(1)}, u32[]{:S(2)}) copy-start(s32[1,8192]{1,0:T(1,128)S(1)} %get-tuple-element.247.seg_ref) | copy-start | bytes 98308
  52.7 3.7 collective-permute-start.1
  66.8 66.1 %all-to-all-start = ((bf16[16,192,512]{2,1,0:T(8,128)(2,1)}), bf16[16,192,512]{2,1,0:T(8,128)(2,1)S(1)}, u32[]{:S(2)}, u32[]{:S(2)}) async-start(bf16[16,192,512]{2,1,0:T(8,128)(2,1)} %pad_maximum_fusion.6), calls=%async_computation | async-start | bytes 6291456 | tf_op jit(solution)/shard_map/all_to_all | solution.py:516
  85.5 125.7 %collective-permute-start.6 = (bf16[656,1024]{1,0:T(8,128)(2,1)}, bf16[656,1024]{1,0:T(8,128)(2,1)}, u32[]{:S(2)}, u32[]{:S(2)}) collective-permute-start(bf16[656,1024]{1,0:T(8,128)(2,1)} %constant_dynamic-slice_fusion.3), channel_id=1, source_target_pairs={{0,1},{1,0},{2,3},{3,2},{4,5},{5,4},{6,7},{7,6},{8,9},{9,8},{10,11... | collective-permute-start | bytes 4030472 | tf_op jit(solution)/shard_map/ppermute | solution.py:236
  87.0 136.4 %collective-permute-start.4 = (bf16[256,5248]{1,0:T(8,128)(2,1)}, bf16[256,5248]{1,0:T(8,128)(2,1)}, u32[]{:S(2)}, u32[]{:S(2)}) collective-permute-start(bf16[256,5248]{1,0:T(8,128)(2,1)} %constant_dynamic-slice_fusion.4), channel_id=1, source_target_pairs={{0,1},{1,0},{2,3},{3,2},{4,5},{5,4},{6,7},{7,6},{8,9},{9,8},{10,11... | collective-permute-start | bytes 8060936 | tf_op jit(solution)/shard_map/ppermute | solution.py:236
  87.5 136.3 %collective-permute-start.2 = (bf16[256,1024]{1,0:T(8,128)(2,1)}, bf16[256,1024]{1,0:T(8,128)(2,1)}, u32[]{:S(2)}, u32[]{:S(2)}) collective-permute-start(bf16[256,1024]{1,0:T(8,128)(2,1)} %constant_dynamic-slice_fusion.5), channel_id=1, source_target_pairs={{0,1},{1,0},{2,3},{3,2},{4,5},{5,4},{6,7},{7,6},{8,9},{9,8},{10,11... | collective-permute-start | bytes 1572872 | tf_op jit(solution)/shard_map/ppermute | solution.py:236
  132.9 78.7 %all-to-all-start.2 = ((bf16[16,192,512]{2,1,0:T(8,128)(2,1)}), bf16[16,192,512]{2,1,0:T(8,128)(2,1)}, u32[]{:S(2)}, u32[]{:S(2)}) async-start(bf16[16,192,512]{2,1,0:T(8,128)(2,1)} %pad_maximum_fusion.7), calls=%async_computation.2 | async-start | bytes 6291456 | tf_op jit(solution)/shard_map/all_to_all | solution.py:516
  211.2 64.5 %collective-permute-start.7 = (bf16[656,1024]{1,0:T(8,128)(2,1)}, bf16[656,1024]{1,0:T(8,128)(2,1)}, u32[]{:S(2)}, u32[]{:S(2)}) collective-permute-start(bf16[656,1024]{1,0:T(8,128)(2,1)} %collective-permute-done.6), channel_id=1, source_target_pairs={{0,2},{2,0},{4,6},{6,4},{8,10},{10,8},{12,14},{14,12},{16,18},{18,... | collective-permute-start | bytes 4030472 | tf_op jit(solution)/shard_map/ppermute | solution.py:236
  211.6 70.5 %all-to-all-start.1 = ((bf16[16,64,512]{2,1,0:T(8,128)(2,1)}), bf16[16,64,512]{2,1,0:T(8,128)(2,1)}, u32[]{:S(2)}, u32[]{:S(2)}) async-start(bf16[16,64,512]{2,1,0:T(8,128)(2,1)} %copy-done.5), calls=%async_computation.1 | async-start | bytes 2097152 | tf_op jit(solution)/shard_map/all_to_all | solution.py:519
  223.3 539.0 %all-gather.6.cloned.1.call-start = ((), (), s32[]{:S(2)}) async-start(), calls=%async_computation.10 | async-start | bytes 35651584 | tf_op jit(solution)/shard_map/all_gather | solution.py:565
  223.4 69.8 %collective-permute-start.5 = (bf16[256,5248]{1,0:T(8,128)(2,1)}, bf16[256,5248]{1,0:T(8,128)(2,1)}, u32[]{:S(2)}, u32[]{:S(2)}) collective-permute-start(bf16[256,5248]{1,0:T(8,128)(2,1)} %collective-permute-done.4), channel_id=1, source_target_pairs={{0,2},{2,0},{4,6},{6,4},{8,10},{10,8},{12,14},{14,12},{16,18},{18,... | collective-permute-start | bytes 8060936 | tf_op jit(solution)/shard_map/ppermute | solution.py:236
  223.8 48.8 %collective-permute-start.3 = (bf16[256,1024]{1,0:T(8,128)(2,1)}, bf16[256,1024]{1,0:T(8,128)(2,1)S(1)}, u32[]{:S(2)}, u32[]{:S(2)}) collective-permute-start(bf16[256,1024]{1,0:T(8,128)(2,1)} %collective-permute-done.2), channel_id=1, source_target_pairs={{0,2},{2,0},{4,6},{6,4},{8,10},{10,8},{12,14},{14,12},{16,18},{18,... | collective-permute-start | bytes 1572872 | tf_op jit(solution)/shard_map/ppermute | solution.py:236
  282.1 84.6 %all-to-all-start.3 = ((bf16[16,64,512]{2,1,0:T(8,128)(2,1)}), bf16[16,64,512]{2,1,0:T(8,128)(2,1)}, u32[]{:S(2)}, u32[]{:S(2)}) async-start(bf16[16,64,512]{2,1,0:T(8,128)(2,1)} %get-tuple-element.65), calls=%async_computation.3 | async-start | bytes 2097152 | tf_op jit(solution)/shard_map/all_to_all | solution.py:519
  370.5 100.7 %all-to-all-start.4 = ((bf16[16,64,512]{2,1,0:T(8,128)(2,1)}), bf16[16,64,512]{2,1,0:T(8,128)(2,1)}, u32[]{:S(2)}, u32[]{:S(2)}) async-start(bf16[16,64,512]{2,1,0:T(8,128)(2,1)} %bitcast.242), calls=%async_computation.4 | async-start | bytes 2097152 | tf_op jit(solution)/shard_map/all_to_all | solution.py:516
  510.4 25.8 %collective-permute-start.8 = (bf16[1504,32,128]{2,1,0:T(8,128)(2,1)}, bf16[1504,32,128]{2,1,0:T(8,128)(2,1)}, u32[]{:S(2)}, u32[]{:S(2)}) collective-permute-start(bf16[1504,32,128]{2,1,0:T(8,128)(2,1)} %get-tuple-element.76), channel_id=1, source_target_pairs={{0,2},{2,0},{4,6},{6,4},{8,10},{10,8},{12,14},{14,12},{16,18},{18,... | collective-permute-start | bytes 36962312 | tf_op jit(solution)/shard_map/ppermute | solution.py:236
  530.1 136.9 %all-to-all-start.6 = ((bf16[16,64,512]{2,1,0:T(8,128)(2,1)}), bf16[16,64,512]{2,1,0:T(8,128)(2,1)S(1)}, u32[]{:S(2)}, u32[]{:S(2)}) async-start(bf16[16,64,512]{2,1,0:T(8,128)(2,1)} %bitcast.31), calls=%async_computation.6 | async-start | bytes 2097152 | tf_op jit(solution)/shard_map/all_to_all | solution.py:516
  547.6 111.7 %collective-permute-start.10 = (bf16[376,32,128]{2,1,0:T(8,128)(2,1)}, bf16[376,32,128]{2,1,0:T(8,128)(2,1)}, u32[]{:S(2)}, u32[]{:S(2)}) collective-permute-start(bf16[376,32,128]{2,1,0:T(8,128)(2,1)} %get-tuple-element.192), channel_id=1, source_target_pairs={{0,4},{2,6},{4,0},{6,2},{8,12},{10,14},{12,8},{14,10},{16,20},{18,... | collective-permute-start | bytes 9240584 | tf_op jit(solution)/shard_map/ppermute | solution.py:236
  549.5 109.8 %collective-permute-start.9 = (bf16[376,32,128]{2,1,0:T(8,128)(2,1)}, bf16[376,32,128]{2,1,0:T(8,128)(2,1)}, u32[]{:S(2)}, u32[]{:S(2)}) collective-permute-start(bf16[376,32,128]{2,1,0:T(8,128)(2,1)} %get-tuple-element.193), channel_id=1, source_target_pairs={{0,1},{1,0},{2,3},{3,2},{4,5},{5,4},{6,7},{7,6},{8,9},{9,8},{10,11... | collective-permute-start | bytes 9240584 | tf_op jit(solution)/shard_map/ppermute | solution.py:236
  663.1 91.0 %collective-permute-start.11 = (bf16[188,32,128]{2,1,0:T(8,128)(2,1)}, bf16[188,32,128]{2,1,0:T(8,128)(2,1)}, u32[]{:S(2)}, u32[]{:S(2)}) collective-permute-start(bf16[188,32,128]{2,1,0:T(8,128)(2,1)} %get-tuple-element.210), channel_id=1, source_target_pairs={{0,4},{2,6},{4,0},{6,2},{8,12},{10,14},{12,8},{14,10},{16,20},{18,... | collective-permute-start | bytes 4620296 | tf_op jit(solution)/shard_map/ppermute | solution.py:236
  667.1 87.1 %collective-permute-start.12 = (bf16[188,32,128]{2,1,0:T(8,128)(2,1)}, bf16[188,32,128]{2,1,0:T(8,128)(2,1)}, u32[]{:S(2)}, u32[]{:S(2)}) collective-permute-start(bf16[188,32,128]{2,1,0:T(8,128)(2,1)} %get-tuple-element.208), channel_id=1, source_target_pairs={{0,1},{1,0},{2,3},{3,2},{4,5},{5,4},{6,7},{7,6},{8,9},{9,8},{10,11... | collective-permute-start | bytes 4620296 | tf_op jit(solution)/shard_map/ppermute | solution.py:236
  668.0 113.1 %all-to-all-start.5 = ((bf16[16,192,512]{2,1,0:T(8,128)(2,1)}), bf16[16,192,512]{2,1,0:T(8,128)(2,1)S(1)}, u32[]{:S(2)}, u32[]{:S(2)}) async-start(bf16[16,192,512]{2,1,0:T(8,128)(2,1)} %get-tuple-element.81), calls=%async_computation.5 | async-start | bytes 6291456 | tf_op jit(solution)/shard_map/all_to_all | solution.py:519
  760.3 46.3 %collective-permute-start.14 = (bf16[2,94,32,128]{3,2,1,0:T(8,128)(2,1)}, bf16[2,94,32,128]{3,2,1,0:T(8,128)(2,1)}, u32[]{:S(2)}, u32[]{:S(2)}) collective-permute-start(bf16[2,94,32,128]{3,2,1,0:T(8,128)(2,1)} %pad_maximum_fusion.13), channel_id=1, source_target_pairs={{0,8},{2,10},{4,12},{6,14},{8,0},{10,2},{12,4},{14,6},{16,24},{18,... | collective-permute-start | bytes 4620296 | tf_op jit(solution)/shard_map/ppermute | solution.py:236
  781.1 24.2 %collective-permute-start.13 = (bf16[192,1024]{1,0:T(8,128)(2,1)}, bf16[192,1024]{1,0:T(8,128)(2,1)}, u32[]{:S(2)}, u32[]{:S(2)}) collective-permute-start(bf16[192,1024]{1,0:T(8,128)(2,1)} %get-tuple-element.95), channel_id=1, source_target_pairs={{0,1},{1,0},{2,3},{3,2},{4,5},{5,4},{6,7},{7,6},{8,9},{9,8},{10,11... | collective-permute-start | bytes 1179656 | tf_op jit(solution)/shard_map/ppermute | solution.py:236
  808.6 66.4 %all-to-all-start.7 = ((bf16[16,8,32,128]{3,2,1,0:T(8,128)(2,1)}), bf16[16,8,32,128]{3,2,1,0:T(8,128)(2,1)S(1)}, u32[]{:S(2)}, u32[]{:S(2)}) async-start(bf16[16,8,32,128]{3,2,1,0:T(8,128)(2,1)} %bitcast.235), calls=%async_computation.7 | async-start | bytes 2097152 | tf_op jit(solution)/shard_map/all_to_all | solution.py:465
  814.8 58.1 %collective-permute-start.15 = (bf16[94,32,128]{2,1,0:T(8,128)(2,1)S(1)}, bf16[94,32,128]{2,1,0:T(8,128)(2,1)S(1)}, u32[]{:S(2)}, u32[]{:S(2)}) collective-permute-start(bf16[94,32,128]{2,1,0:T(8,128)(2,1)S(1)} %fusion.93), channel_id=1, source_target_pairs={{0,16},{2,18},{4,20},{6,22},{8,24},{10,26},{12,28},{14,30},{16,0},... | collective-permute-start | bytes 2310152 | tf_op jit(solution)/shard_map/ppermute | solution.py:236
  884.9 75.0 %all-to-all-start.8 = ((bf16[16,192,512]{2,1,0:T(8,128)(2,1)}), bf16[16,192,512]{2,1,0:T(8,128)(2,1)}, u32[]{:S(2)}, u32[]{:S(2)}) async-start(bf16[16,192,512]{2,1,0:T(8,128)(2,1)} %get-tuple-element.98), calls=%async_computation.8 | async-start | bytes 6291456 | tf_op jit(solution)/shard_map/all_to_all | solution.py:519
  959.9 13.6 %collective-permute-start.16 = (f32[2,1024]{1,0:T(2,128)S(1)}, f32[2,1024]{1,0:T(2,128)S(1)}, u32[]{:S(2)}, u32[]{:S(2)}) collective-permute-start(f32[2,1024]{1,0:T(2,128)S(1)} %pad_maximum_fusion.16), channel_id=1, source_target_pairs={{0,2},{2,0},{4,6},{6,4},{8,10},{10,8},{12,14},{14,12},{16,18},{18,... | collective-permute-start | bytes 24584 | tf_op jit(solution)/shard_map/ppermute | solution.py:236
  973.5 3.7 collective-permute-start.17
  977.2 3.7 collective-permute-start.18
  980.8 4.9 collective-permute-start.19
  985.8 7.6 collective-permute-start.20
  (110 other events, 1696.7 us)
Sparse Core Ops, SparseCore 0:
  226.3 213.0 all-gather.5

commit v2 on v1

--- a/solution.py
+++ b/solution.py
@@ -331,7 +331,7 @@
     )(where, *grads)
 
 
-def soap_kernel(block, kind_ref, pick_ref, live_ref, pool, early, master, first, second, left, right,
+def soap_kernel(block, kind_ref, pick_ref, live_ref, pool, rest, early, master, first, second, left, right,
                 grads_out, master_out, copy_out, first_out, second_out, tiles, sem):
     step = pl.program_id(0)
     total = tiles.shape[0]
@@ -339,7 +339,16 @@
     @pl.when(step == 0)
     def _():
         def fetch(n, carry):
-            pltpu.make_async_copy(pool.at[pick_ref[n]], tiles.at[n], sem).start()
+            pick = pick_ref[n]
+
+            @pl.when(pick < pool.shape[0])
+            def _():
+                pltpu.make_async_copy(pool.at[pick], tiles.at[n], sem).start()
+
+            @pl.when(pick >= pool.shape[0])
+            def _():
+                pltpu.make_async_copy(rest.at[pick - pool.shape[0]], tiles.at[n], sem).start()
+
             return carry
 
         lax.fori_loop(0, total, fetch, 0)
@@ -387,7 +396,7 @@
             second_out[k] = jnp.where(live, s, second[k])
 
 
-def soap_step(picks, pool, early, master, first, second, left, right):
+def soap_step(picks, pools, early, master, first, second, left, right):
     cap = master.shape[0]
     block = min(16, cap)
     spec = pl.BlockSpec((block, 64, 64), lambda i: (i, 0, 0))
@@ -397,13 +406,13 @@
         functools.partial(soap_kernel, block),
         grid=(-(-cap // block),),
         out_shape=(like, like, jax.ShapeDtypeStruct(master.shape, BF), like, like),
-        in_specs=[SM] * 3 + [whole, pl.BlockSpec((block, 32, 128), lambda i: (i, 0, 0))] + [spec] * 5,
+        in_specs=[SM] * 3 + [whole] * 2 + [pl.BlockSpec((block, 32, 128), lambda i: (i, 0, 0))] + [spec] * 5,
         out_specs=(spec,) * 5,
         scratch_shapes=[pltpu.VMEM((cap, 32, 128), BF), pltpu.SemaphoreType.DMA],
         compiler_params=pltpu.CompilerParams(vmem_limit_bytes=40 << 20),
         cost_estimate=pl.CostEstimate(flops=23 << 30, bytes_accessed=30 << 20, transcendentals=0),
         name="soap",
-    )(*picks, pool, early, master, first, second, left, right)
+    )(*picks, *pools, early, master, first, second, left, right)
 
 
 def own_tiles(slot_table, slot_cap):
@@ -474,7 +483,7 @@
     own_rank = rank.reshape(-1)[jnp.clip(head * per + part * across + row, 0, heads * per - 1)]
     early = own_rank < ROUND
     place = jnp.where(early, head * ROUND + own_rank, ctx_size * ROUND + own)
-    return jnp.concatenate([got.reshape(-1, 32, 128), rest], axis=0), place, got
+    return (got.reshape(-1, 32, 128), rest), place, got
 
 
 def gain_step(grads_in, gains_old, first_old, second_old):
@@ -674,10 +683,10 @@
     if fast and heads == ctx_size:
         grad_heads = after(grad_heads + swap_bit(grad_heads, "fsdp", 1), first_turn)
         pool, place, first_round = send_tiles(slot_table, slot_cap, grad_heads, own)
-        last_grads = after(last_grads, first_round, own_slots, pool, *outputs_list)
+        last_grads = after(last_grads, first_round, own_slots, pool[1], *outputs_list)
     else:
         grad_heads = lax.psum(grad_heads, "fsdp")
-        pool = all_tiles(lax.all_gather(grad_heads[None], "ctx", axis=0, tiled=True)[::copies])
+        pool = (all_tiles(lax.all_gather(grad_heads[None], "ctx", axis=0, tiled=True)[::copies]),) * 2
         place = own
     d_proj_all.append(collect(last_grads))
     picks = (is_qkv.astype(jnp.int32), jnp.where(is_qkv, place, 0), live)

time: 1020 us -> 1010 us (level); the launches traced: 1000 us -> 1010 us
  Pallas kernels: 345 us -> 378 us
  starting transfers between devices: 123 us -> 98.1 us
    ppermute x21, starting transfers between devices: 55 us -> 30.1 us  [swap_bit(): return lax.ppermute(x, axis, [(s, s ^ bit) for s in range(n)])]
    pallas_call x2, Pallas kernels: 177 us -> 196 us  [attend_backward(): pl.pallas_call(functools.partial(bwd_kernel, bq, bk, sub), out_shape=(jax...]
    pallas_call x2, Pallas kernels: 108 us -> 123 us  [attend_forward(): pl.pallas_call(functools.partial(fwd_kernel, bq, bk, sub), out_shape=(jax...]
    unnamed x233 -> x237, local copies, waits for them, and re-layouts: 63.8 us -> 64.6 us
  transfers between devices with their start and end apart: 31 -> 31, of which waited for: 7 -> 8; matrix products, arithmetic and copies ran while one was open for 34% -> 34% of each run, Pallas kernels for 34% -> 37%
where the time goes in v2:
time: 1010 us
  Pallas kernels  378 us (37%)
  matrix products  165 us (16%)
  other arithmetic  130 us (13%)
  starting transfers between devices  98.1 us (10%)
  waiting for transfers between devices  96.7 us (10%)
  local copies, waits for them, and re-layouts  90.9 us (9%)
  blocking collectives  33.9 us (3%)
  between operations  16.6 us (2%)
    pallas_call x2, Pallas kernels, attend_backward(): pl.pallas_call(functools.partial(bwd_kernel, bq, bk, sub), out_shape=(jax...  196 us
    dot_general x21, matrix products, mm(): lax.dot_general(a, b, (((da,), (db,)), ((), ())), preferred_element_type=...  165 us
    pallas_call x2, Pallas kernels, attend_forward(): pl.pallas_call(functools.partial(fwd_kernel, bq, bk, sub), out_shape=(jax...  123 us
    unnamed x237, local copies, waits for them, and re-layouts  64.6 us
    ppermute x21, waiting for transfers between devices, swap_bit(): return lax.ppermute(x, axis, [(s, s ^ bit) for s in range(n)])  61.7 us
    pallas_call x1, Pallas kernels, scatter_tiles(): pl.pallas_call(functools.partial(scatter_kernel, counts, parts), out_shap...  38.9 us
    all_to_all x4, waiting for transfers between devices, spread(): return lax.all_to_all(x, 'ctx', 0, 0, tiled=True)  34.8 us
    all_gather x1, blocking collectives, on_device(): gains = lax.all_gather(norm_gains, 'fsdp', axis=1, tiled=True).astype(F32)  33.9 us
  transfers between devices with their start and end apart: 31, of which 8 were waited for; matrix products, arithmetic and copies ran while one was open for 34% of the time, Pallas kernels for 37%

profile of v2, /device:TPU:0, one launch (start us, length us, event | category | flops | bytes accessed | tf_op | source)
XLA Modules:
  0.0 1009.7 jit_solution(8668237958352241596)
XLA Ops:
  18.4 33.9 %all_gather.9 = bf16[2,1024]{1,0:T(2,128)(2,1)S(1)} all-gather(bf16[2,512]{1,0:T(2,128)(2,1)S(1)} %copy-done.110), channel_id=1, replica_groups=mesh['ctx'=16,'fsdp'=2] {'fsdp'}, dimensions={1}, use_global_device_ids=true | all-gather | bytes 6144 | tf_op jit(solution)/shard_map/all_gather | solution.py:531
  66.7 6.5 all-to-all-start
  97.8 34.8 %all-to-all-done.qkv_ref = bf16[16,192,512]{2,1,0:T(8,128)(2,1)S(1)} async-done(((bf16[16,192,512]{2,1,0:T(8,128)(2,1)}), bf16[16,192,512]{2,1,0:T(8,128)(2,1)S(1)}, u32[]{:S(2)}, u32[]{:S(2)}) %all-to-all-start) | async-done | bytes 3145760 | tf_op jit(solution)/shard_map/all_to_all | solution.py:525
  132.6 15.5 %all-to-all-start.2 = ((bf16[16,192,512]{2,1,0:T(8,128)(2,1)}), bf16[16,192,512]{2,1,0:T(8,128)(2,1)}, u32[]{:S(2)}, u32[]{:S(2)}) async-start(bf16[16,192,512]{2,1,0:T(8,128)(2,1)} %pad_maximum_fusion.6), calls=%async_computation.2 | async-start | bytes 6291456 | tf_op jit(solution)/shard_map/all_to_all | solution.py:525
  148.1 60.7 %attend_fwd.2 = (bf16[16,64,512]{2,1,0:T(8,128)(2,1)S(1)}, f32[64,8192]{1,0:T(8,128)S(1)}, f32[1,8192]{1,0:T(1,128)S(1)}) custom-call(s32[8]{0:T(128)S(1)} %get-tuple-element.276.lo_ref, s32[8]{0:T(128)S(1)} %get-tuple-element.278.hi_ref, bf16[16,192,512]{2,1,0:T(8,128)(2,1)S(1)} %all-to-all-done.qkv_ref, s32[1,8192]{1,0:T(1,128)S(1)} %get-tuple-element.246.seg_ref), custom_call_target="tpu_custom_call" | custom-call | flops 76504104960 | bytes 8388608 | tf_op jit(solution)/shard_map/attend_fwd/pallas_call | solution.py:157
  212.2 10.8 %all-to-all-start.1 = ((bf16[16,64,512]{2,1,0:T(8,128)(2,1)}), bf16[16,64,512]{2,1,0:T(8,128)(2,1)}, u32[]{:S(2)}, u32[]{:S(2)}) async-start(bf16[16,64,512]{2,1,0:T(8,128)(2,1)} %copy-done.7), calls=%async_computation.1 | async-start | bytes 2097152 | tf_op jit(solution)/shard_map/all_to_all | solution.py:528
  223.8 62.3 %attend_fwd.3 = (bf16[16,64,512]{2,1,0:T(8,128)(2,1)}, f32[64,8192]{1,0:T(8,128)S(1)}, f32[1,8192]{1,0:T(1,128)S(1)}) custom-call(s32[8]{0:T(128)S(1)} %get-tuple-element.275.lo_ref, s32[8]{0:T(128)S(1)} %get-tuple-element.277.hi_ref, bf16[16,192,512]{2,1,0:T(8,128)(2,1)} %all-to-all-done.2.qkv_ref, s32[1,8192]{1,0:T(1,128)S(1)} %get-tuple-element.247.seg_ref), custom_call_target="tpu_custom_call" | custom-call | flops 76504104960 | bytes 8388608 | tf_op jit(solution)/shard_map/attend_fwd/pallas_call | solution.py:157
  317.1 8.2 fusion.139
  325.4 13.5 %multiply_convert_fusion.1 = (bf16[512,2624]{1,0:T(8,128)(2,1)}, f32[512,2624]{1,0:T(8,128)S(1)}) fusion(f32[512,5248]{1,0:T(8,128)S(1)} %fusion.139), kind=kLoop, calls=%fused_computation.40 | loop fusion | flops 88670208 | bytes 18808832 | tf_op jit(solution)/shard_map/convert_element_type | solution.py:593
  338.8 13.0 %bitcast_multiply_fusion.3 = (f32[512,2624]{1,0:T(8,128)}, f32[512,2624]{1,0:T(8,128)}) fusion(f32[512,2624]{1,0:T(8,128)S(1)} %get-tuple-element.189, f32[512,5248]{1,0:T(8,128)} %copy-done.38, bf16[2,512,1024]{2,1,0:T(8,128)(2,1)S(1)} %copy-done.39, bf16[1312,1024]{1,0:T(8,128)(2,1)} %get-tuple-element.213, bf16[1312,1024]{1,0:T(8,128)(2,1)} %get-tuple-element.212), kind=kOutput, calls=%fused_computation.24 | convolution fusion | flops 2783707136 | bytes 33423360 | tf_op jit(solution)/shard_map/dot_general | solution.py:227
  351.9 8.1 add_convert_fusion.1
  359.9 14.6 %multiply_reduce_fusion.1 = (f32[1024]{0:T(1024)}, f32[512]{0:T(512)S(1)}, f32[512,1024]{1,0:T(8,128)}) fusion(f32[512,1024]{1,0:T(8,128)} %copy-done.21, f32[512]{0:T(512)S(1)} %fusion.117, f32[512]{0:T(512)S(1)} %broadcast_multiply_fusion.1, f32[1024]{0:T(1024)S(1)} %bitcast.246, bf16[512,5248]{1,0:T(8,128)(2,1)} %add_convert_fusion.1, ...), kind=kOutput, calls=%fused_computation.134 | convolution fusion | flops 5528091136 | bytes 20330496 | tf_op jit(solution)/shard_map/dot_general | solution.py:227
  395.4 9.2 fusion.137
  404.6 18.2 %bitcast_multiply_fusion.1 = (f32[512,2624]{1,0:T(8,128)}, f32[512,2624]{1,0:T(8,128)S(1)}, f32[2624,512]{0,1:T(8,128)}) fusion(f32[512,5248]{1,0:T(8,128)S(1)} %fusion.137, bf16[2,512,1024]{2,1,0:T(8,128)(2,1)S(1)} %copy-done.41, bf16[1312,1024]{1,0:T(8,128)(2,1)} %get-tuple-element.213, bf16[1312,1024]{1,0:T(8,128)(2,1)S(1)} %copy-done.55), kind=kOutput, calls=%fused_computation.22 | convolution fusion | flops 2849538048 | bytes 28049408 | tf_op jit(solution)/shard_map/dot_general | solution.py:227
  422.8 7.6 multiply_add_fusion
  430.4 8.1 add_convert_fusion
  438.6 11.6 %multiply_reduce_fusion = (f32[1024]{0:T(1024)}, f32[512]{0:T(512)S(1)}, f32[512,1024]{1,0:T(8,128)S(1)}) fusion(f32[512,1024]{1,0:T(8,128)S(1)} %copy-done.25, f32[512]{0:T(512)S(1)} %fusion.118, f32[512]{0:T(512)S(1)} %broadcast_multiply_fusion, f32[1024]{0:T(1024)S(1)} %bitcast.249, bf16[512,5248]{1,0:T(8,128)(2,1)} %add_convert_fusion, ...), kind=kOutput, calls=%fused_computation.133 | convolution fusion | flops 5528091136 | bytes 20330496 | tf_op jit(solution)/shard_map/dot_general | solution.py:227
  453.3 18.6 %convolution_convert_fusion.refs_1_ = bf16[1024,5248]{1,0:T(8,128)(2,1)} fusion(bf16[512,5248]{1,0:T(8,128)(2,1)} %add_convert_fusion, bf16[512,5248]{1,0:T(8,128)(2,1)} %add_convert_fusion.1, bf16[512,1024]{1,0:T(8,128)(2,1)S(1)} %copy-done.69, bf16[512,1024]{1,0:T(8,128)(2,1)S(1)} %copy-done.67), kind=kOutput, calls=%fused_computation.5 | convolution fusion | flops 11036917760 | bytes 23592960 | tf_op jit(solution)/shard_map/dot_general | solution.py:227
  476.3 7.8 convolution_convert_fusion.1.refs_2_
  484.2 38.9 %scatter_tiles.1 = (bf16[1504,32,128]{2,1,0:T(8,128)(2,1)}, bf16[1504,32,128]{2,1,0:T(8,128)(2,1)}) custom-call(s32[2224]{0:T(1024)S(1)} %select_add_fusion.where_ref, bf16[1024,1024]{1,0:T(8,128)(2,1)S(1)} %fusion.60.refs_0_, bf16[1024,5248]{1,0:T(8,128)(2,1)} %convolution_convert_fusion.refs_1_, bf16[2624,1024]{1,0:T(8,128)(2,1)} %convolution_convert_fusion.1.refs_2_), custom_call_target="tpu_custom_call" | custom-call | flops 42949672960 | bytes 41943040 | tf_op jit(solution)/shard_map/scatter_tiles/pallas_call | solution.py:322
  532.0 8.9 multiply_sine_fusion
  548.9 11.4 %slice_add_fusion = (bf16[376,32,128]{2,1,0:T(8,128)(2,1)}, bf16[376,32,128]{2,1,0:T(8,128)(2,1)}, bf16[376,32,128]{2,1,0:T(8,128)(2,1)S(1)}, bf16[376,32,128]{2,1,0:T(8,128)(2,1)S(1)}) fusion(bf16[1504,32,128]{2,1,0:T(8,128)(2,1)} %collective-permute-done.8, bf16[1504,32,128]{2,1,0:T(8,128)(2,1)} %get-tuple-element.75), kind=kLoop, calls=%fused_computation.78 | loop fusion | flops 6160384 | bytes 36962304 | tf_op jit(solution)/shard_map/add | solution.py:639
  562.4 99.5 %attend_bwd.2 = (bf16[16,192,512]{2,1,0:T(8,128)(2,1)}, bf16[192,8192]{1,0:T(8,128)(2,1)}) custom-call(s32[16]{0:T(128)} %get-tuple-element.273.lo_ref, s32[16]{0:T(128)} %get-tuple-element.274.hi_ref, bf16[16,192,512]{2,1,0:T(8,128)(2,1)} %copy-done, s32[1,8192]{1,0:T(1,128)} %copy-done.9, bf16[16,64,512]{2,1,0:T(8,128)(2,1)} %all-to-all-done.4.do_ref, ...), custom_call_target="tpu_custom_call" | custom-call | flops 106032005120 | bytes 16777216 | tf_op jit(solution)/shard_map/attend_bwd/pallas_call | solution.py:167
  669.7 7.5 collective-permute-start.12
  678.1 6.4 all-to-all-start.5
  684.5 96.9 %attend_bwd.3 = (bf16[16,192,512]{2,1,0:T(8,128)(2,1)}, bf16[192,8192]{1,0:T(8,128)(2,1)}) custom-call(s32[16]{0:T(128)} %get-tuple-element.271.lo_ref, s32[16]{0:T(128)} %get-tuple-element.272.hi_ref, bf16[16,192,512]{2,1,0:T(8,128)(2,1)} %all-to-all-done.2.qkv_ref, s32[1,8192]{1,0:T(1,128)} %copy-done.8, bf16[16,64,512]{2,1,0:T(8,128)(2,1)} %copy-done.70, ...), custom_call_target="tpu_custom_call" | custom-call | flops 106032005120 | bytes 16777216 | tf_op jit(solution)/shard_map/attend_bwd/pallas_call | solution.py:167
  789.6 8.6 fusion
  798.3 10.1 %fusion.88 = (f32[1024]{0:T(1024)S(1)}, bf16[192,1024]{1,0:T(8,128)(2,1)}) fusion(bf16[1024,3,1,64]{0,3,2,1:T(8,128)(2,1)S(1)} %copy-done.71, f32[192,1024]{1,0:T(8,128)S(1)} %fusion, bf16[192,8192]{1,0:T(8,128)(2,1)S(1)} %copy-done.111, bf16[2,8192,1024]{2,1,0:T(8,128)(2,1)} %all-gather.6.cloned.1.call-done), kind=kOutput, calls=%fused_computation.200 | convolution fusion | flops 3222207488 | bytes 21499904 | tf_op jit(solution)/shard_map/dot_general | solution.py:227
  811.3 8.4 collective-permute-done.13
  836.1 7.5 add_convert_fusion.5
  847.8 43.5 %collective-permute-done.15 = bf16[94,32,128]{2,1,0:T(8,128)(2,1)S(1)} collective-permute-done((bf16[94,32,128]{2,1,0:T(8,128)(2,1)S(1)}, bf16[94,32,128]{2,1,0:T(8,128)(2,1)S(1)}, u32[]{:S(2)}, u32[]{:S(2)}) %collective-permute-start.15) | collective-permute-done | bytes 770080 | tf_op jit(solution)/shard_map/ppermute | solution.py:236
  930.2 19.2 %soap.1 = (f32[94,64,64]{2,1,0:T(8,128)S(1)}, f32[94,64,64]{2,1,0:T(8,128)S(1)}, bf16[94,64,64]{2,1,0:T(8,128)(2,1)S(1)}, f32[94,64,64]{2,1,0:T(8,128)S(1)}, f32[94,64,64]{2,1,0:T(8,128)}) custom-call(s32[94]{0:T(128)S(1)} %compare_convert_fusion.kind_ref, s32[94]{0:T(128)S(1)} %compare_select_fusion.35.pick_ref, s32[94]{0:T(128)S(1)} %convert_element_type.218.live_ref, ...), custom_call_target="tpu_custom_call" | custom-call | flops 24696061952 | bytes 31457280 | tf_op jit(solution)/shard_map/soap/pallas_call | solution.py:405
  (437 shorter events, 266.6 us)
Async XLA Ops:
  14.6 38.1 %collective-permute-start = (bf16[256,3072]{0,1:T(8,128)(2,1)}, bf16[256,3072]{0,1:T(8,128)(2,1)}, u32[]{:S(2)}, u32[]{:S(2)}) collective-permute-start(bf16[256,3072]{0,1:T(8,128)(2,1)} %constant_dynamic-slice_fusion.6), channel_id=1, source_target_pairs={{0,1},{1,0},{2,3},{3,2},{4,5},{5,4},{6,7},{7,6},{8,9},{9,8},{10,11... | collective-permute-start | bytes 4718600 | tf_op jit(solution)/shard_map/ppermute | solution.py:236
  17.7 508.2 %copy-start.8 = (s32[1,8192]{1,0:T(1,128)}, s32[1,8192]{1,0:T(1,128)S(1)}, u32[]{:S(2)}) copy-start(s32[1,8192]{1,0:T(1,128)S(1)} %get-tuple-element.247.seg_ref) | copy-start | bytes 98308
  52.7 3.7 collective-permute-start.1
  66.7 65.9 %all-to-all-start = ((bf16[16,192,512]{2,1,0:T(8,128)(2,1)}), bf16[16,192,512]{2,1,0:T(8,128)(2,1)S(1)}, u32[]{:S(2)}, u32[]{:S(2)}) async-start(bf16[16,192,512]{2,1,0:T(8,128)(2,1)} %pad_maximum_fusion.5), calls=%async_computation | async-start | bytes 6291456 | tf_op jit(solution)/shard_map/all_to_all | solution.py:525
  85.2 126.6 %collective-permute-start.6 = (bf16[656,1024]{1,0:T(8,128)(2,1)}, bf16[656,1024]{1,0:T(8,128)(2,1)}, u32[]{:S(2)}, u32[]{:S(2)}) collective-permute-start(bf16[656,1024]{1,0:T(8,128)(2,1)} %constant_dynamic-slice_fusion.3), channel_id=1, source_target_pairs={{0,1},{1,0},{2,3},{3,2},{4,5},{5,4},{6,7},{7,6},{8,9},{9,8},{10,11... | collective-permute-start | bytes 4030472 | tf_op jit(solution)/shard_map/ppermute | solution.py:236
  86.7 136.4 %collective-permute-start.4 = (bf16[256,5248]{1,0:T(8,128)(2,1)}, bf16[256,5248]{1,0:T(8,128)(2,1)}, u32[]{:S(2)}, u32[]{:S(2)}) collective-permute-start(bf16[256,5248]{1,0:T(8,128)(2,1)} %constant_dynamic-slice_fusion.4), channel_id=1, source_target_pairs={{0,1},{1,0},{2,3},{3,2},{4,5},{5,4},{6,7},{7,6},{8,9},{9,8},{10,11... | collective-permute-start | bytes 8060936 | tf_op jit(solution)/shard_map/ppermute | solution.py:236
  87.2 136.3 %collective-permute-start.2 = (bf16[256,1024]{1,0:T(8,128)(2,1)}, bf16[256,1024]{1,0:T(8,128)(2,1)}, u32[]{:S(2)}, u32[]{:S(2)}) collective-permute-start(bf16[256,1024]{1,0:T(8,128)(2,1)} %constant_dynamic-slice_fusion.5), channel_id=1, source_target_pairs={{0,1},{1,0},{2,3},{3,2},{4,5},{5,4},{6,7},{7,6},{8,9},{9,8},{10,11... | collective-permute-start | bytes 1572872 | tf_op jit(solution)/shard_map/ppermute | solution.py:236
  132.6 79.5 %all-to-all-start.2 = ((bf16[16,192,512]{2,1,0:T(8,128)(2,1)}), bf16[16,192,512]{2,1,0:T(8,128)(2,1)}, u32[]{:S(2)}, u32[]{:S(2)}) async-start(bf16[16,192,512]{2,1,0:T(8,128)(2,1)} %pad_maximum_fusion.6), calls=%async_computation.2 | async-start | bytes 6291456 | tf_op jit(solution)/shard_map/all_to_all | solution.py:525
  211.8 77.4 %collective-permute-start.7 = (bf16[656,1024]{1,0:T(8,128)(2,1)}, bf16[656,1024]{1,0:T(8,128)(2,1)}, u32[]{:S(2)}, u32[]{:S(2)}) collective-permute-start(bf16[656,1024]{1,0:T(8,128)(2,1)} %collective-permute-done.6), channel_id=1, source_target_pairs={{0,2},{2,0},{4,6},{6,4},{8,10},{10,8},{12,14},{14,12},{16,18},{18,... | collective-permute-start | bytes 4030472 | tf_op jit(solution)/shard_map/ppermute | solution.py:236
  212.2 83.3 %all-to-all-start.1 = ((bf16[16,64,512]{2,1,0:T(8,128)(2,1)}), bf16[16,64,512]{2,1,0:T(8,128)(2,1)}, u32[]{:S(2)}, u32[]{:S(2)}) async-start(bf16[16,64,512]{2,1,0:T(8,128)(2,1)} %copy-done.7), calls=%async_computation.1 | async-start | bytes 2097152 | tf_op jit(solution)/shard_map/all_to_all | solution.py:528
  223.0 566.6 %all-gather.6.cloned.1.call-start = ((), (), s32[]{:S(2)}) async-start(), calls=%async_computation.10 | async-start | bytes 35651584 | tf_op jit(solution)/shard_map/all_gather | solution.py:574
  223.1 83.4 %collective-permute-start.5 = (bf16[256,5248]{1,0:T(8,128)(2,1)}, bf16[256,5248]{1,0:T(8,128)(2,1)}, u32[]{:S(2)}, u32[]{:S(2)}) collective-permute-start(bf16[256,5248]{1,0:T(8,128)(2,1)} %collective-permute-done.4), channel_id=1, source_target_pairs={{0,2},{2,0},{4,6},{6,4},{8,10},{10,8},{12,14},{14,12},{16,18},{18,... | collective-permute-start | bytes 8060936 | tf_op jit(solution)/shard_map/ppermute | solution.py:236
  223.5 62.6 %collective-permute-start.3 = (bf16[256,1024]{1,0:T(8,128)(2,1)}, bf16[256,1024]{1,0:T(8,128)(2,1)S(1)}, u32[]{:S(2)}, u32[]{:S(2)}) collective-permute-start(bf16[256,1024]{1,0:T(8,128)(2,1)} %collective-permute-done.2), channel_id=1, source_target_pairs={{0,2},{2,0},{4,6},{6,4},{8,10},{10,8},{12,14},{14,12},{16,18},{18,... | collective-permute-start | bytes 1572872 | tf_op jit(solution)/shard_map/ppermute | solution.py:236
  295.5 84.2 %all-to-all-start.3 = ((bf16[16,64,512]{2,1,0:T(8,128)(2,1)}), bf16[16,64,512]{2,1,0:T(8,128)(2,1)}, u32[]{:S(2)}, u32[]{:S(2)}) async-start(bf16[16,64,512]{2,1,0:T(8,128)(2,1)} %get-tuple-element.65), calls=%async_computation.3 | async-start | bytes 2097152 | tf_op jit(solution)/shard_map/all_to_all | solution.py:528
  383.6 100.6 %all-to-all-start.4 = ((bf16[16,64,512]{2,1,0:T(8,128)(2,1)}), bf16[16,64,512]{2,1,0:T(8,128)(2,1)}, u32[]{:S(2)}, u32[]{:S(2)}) async-start(bf16[16,64,512]{2,1,0:T(8,128)(2,1)} %bitcast.242), calls=%async_computation.4 | async-start | bytes 2097152 | tf_op jit(solution)/shard_map/all_to_all | solution.py:525
  523.1 25.7 %collective-permute-start.8 = (bf16[1504,32,128]{2,1,0:T(8,128)(2,1)}, bf16[1504,32,128]{2,1,0:T(8,128)(2,1)}, u32[]{:S(2)}, u32[]{:S(2)}) collective-permute-start(bf16[1504,32,128]{2,1,0:T(8,128)(2,1)} %get-tuple-element.76), channel_id=1, source_target_pairs={{0,2},{2,0},{4,6},{6,4},{8,10},{10,8},{12,14},{14,12},{16,18},{18,... | collective-permute-start | bytes 36962312 | tf_op jit(solution)/shard_map/ppermute | solution.py:236
  543.1 134.0 %all-to-all-start.6 = ((bf16[16,64,512]{2,1,0:T(8,128)(2,1)}), bf16[16,64,512]{2,1,0:T(8,128)(2,1)S(1)}, u32[]{:S(2)}, u32[]{:S(2)}) async-start(bf16[16,64,512]{2,1,0:T(8,128)(2,1)} %bitcast.31), calls=%async_computation.6 | async-start | bytes 2097152 | tf_op jit(solution)/shard_map/all_to_all | solution.py:525
  560.3 101.6 %collective-permute-start.10 = (bf16[376,32,128]{2,1,0:T(8,128)(2,1)}, bf16[376,32,128]{2,1,0:T(8,128)(2,1)}, u32[]{:S(2)}, u32[]{:S(2)}) collective-permute-start(bf16[376,32,128]{2,1,0:T(8,128)(2,1)} %get-tuple-element.192), channel_id=1, source_target_pairs={{0,4},{2,6},{4,0},{6,2},{8,12},{10,14},{12,8},{14,10},{16,20},{18,... | collective-permute-start | bytes 9240584 | tf_op jit(solution)/shard_map/ppermute | solution.py:236
  562.2 99.7 %collective-permute-start.9 = (bf16[376,32,128]{2,1,0:T(8,128)(2,1)}, bf16[376,32,128]{2,1,0:T(8,128)(2,1)}, u32[]{:S(2)}, u32[]{:S(2)}) collective-permute-start(bf16[376,32,128]{2,1,0:T(8,128)(2,1)} %get-tuple-element.193), channel_id=1, source_target_pairs={{0,1},{1,0},{2,3},{3,2},{4,5},{5,4},{6,7},{7,6},{8,9},{9,8},{10,11... | collective-permute-start | bytes 9240584 | tf_op jit(solution)/shard_map/ppermute | solution.py:236
  665.7 115.7 %collective-permute-start.11 = (bf16[188,32,128]{2,1,0:T(8,128)(2,1)}, bf16[188,32,128]{2,1,0:T(8,128)(2,1)}, u32[]{:S(2)}, u32[]{:S(2)}) collective-permute-start(bf16[188,32,128]{2,1,0:T(8,128)(2,1)} %get-tuple-element.210), channel_id=1, source_target_pairs={{0,4},{2,6},{4,0},{6,2},{8,12},{10,14},{12,8},{14,10},{16,20},{18,... | collective-permute-start | bytes 4620296 | tf_op jit(solution)/shard_map/ppermute | solution.py:236
  669.7 111.8 %collective-permute-start.12 = (bf16[188,32,128]{2,1,0:T(8,128)(2,1)}, bf16[188,32,128]{2,1,0:T(8,128)(2,1)}, u32[]{:S(2)}, u32[]{:S(2)}) collective-permute-start(bf16[188,32,128]{2,1,0:T(8,128)(2,1)} %get-tuple-element.208), channel_id=1, source_target_pairs={{0,1},{1,0},{2,3},{3,2},{4,5},{5,4},{6,7},{7,6},{8,9},{9,8},{10,11... | collective-permute-start | bytes 4620296 | tf_op jit(solution)/shard_map/ppermute | solution.py:236
  678.1 130.3 %all-to-all-start.5 = ((bf16[16,192,512]{2,1,0:T(8,128)(2,1)}), bf16[16,192,512]{2,1,0:T(8,128)(2,1)S(1)}, u32[]{:S(2)}, u32[]{:S(2)}) async-start(bf16[16,192,512]{2,1,0:T(8,128)(2,1)} %get-tuple-element.81), calls=%async_computation.5 | async-start | bytes 6291456 | tf_op jit(solution)/shard_map/all_to_all | solution.py:528
  787.6 36.4 %collective-permute-start.14 = (bf16[2,94,32,128]{3,2,1,0:T(8,128)(2,1)}, bf16[2,94,32,128]{3,2,1,0:T(8,128)(2,1)}, u32[]{:S(2)}, u32[]{:S(2)}) collective-permute-start(bf16[2,94,32,128]{3,2,1,0:T(8,128)(2,1)} %pad_maximum_fusion.12), channel_id=1, source_target_pairs={{0,8},{2,10},{4,12},{6,14},{8,0},{10,2},{12,4},{14,6},{16,24},{18,... | collective-permute-start | bytes 4620296 | tf_op jit(solution)/shard_map/ppermute | solution.py:236
  808.4 11.2 %collective-permute-start.13 = (bf16[192,1024]{1,0:T(8,128)(2,1)}, bf16[192,1024]{1,0:T(8,128)(2,1)}, u32[]{:S(2)}, u32[]{:S(2)}) collective-permute-start(bf16[192,1024]{1,0:T(8,128)(2,1)} %get-tuple-element.95), channel_id=1, source_target_pairs={{0,1},{1,0},{2,3},{3,2},{4,5},{5,4},{6,7},{7,6},{8,9},{9,8},{10,11... | collective-permute-start | bytes 1179656 | tf_op jit(solution)/shard_map/ppermute | solution.py:236
  826.0 67.5 %all-to-all-start.7 = ((bf16[16,8,32,128]{3,2,1,0:T(8,128)(2,1)}), bf16[16,8,32,128]{3,2,1,0:T(8,128)(2,1)S(1)}, u32[]{:S(2)}, u32[]{:S(2)}) async-start(bf16[16,8,32,128]{3,2,1,0:T(8,128)(2,1)} %bitcast.235), calls=%async_computation.7 | async-start | bytes 2097152 | tf_op jit(solution)/shard_map/all_to_all | solution.py:474
  833.3 58.1 %collective-permute-start.15 = (bf16[94,32,128]{2,1,0:T(8,128)(2,1)S(1)}, bf16[94,32,128]{2,1,0:T(8,128)(2,1)S(1)}, u32[]{:S(2)}, u32[]{:S(2)}) collective-permute-start(bf16[94,32,128]{2,1,0:T(8,128)(2,1)S(1)} %fusion.93), channel_id=1, source_target_pairs={{0,16},{2,18},{4,20},{6,22},{8,24},{10,26},{12,28},{14,30},{16,0},... | collective-permute-start | bytes 2310152 | tf_op jit(solution)/shard_map/ppermute | solution.py:236
  897.9 74.0 %all-to-all-start.8 = ((bf16[16,192,512]{2,1,0:T(8,128)(2,1)}), bf16[16,192,512]{2,1,0:T(8,128)(2,1)}, u32[]{:S(2)}, u32[]{:S(2)}) async-start(bf16[16,192,512]{2,1,0:T(8,128)(2,1)} %get-tuple-element.98), calls=%async_computation.8 | async-start | bytes 6291456 | tf_op jit(solution)/shard_map/all_to_all | solution.py:528
  971.8 13.4 %collective-permute-start.16 = (f32[2,1024]{1,0:T(2,128)S(1)}, f32[2,1024]{1,0:T(2,128)S(1)}, u32[]{:S(2)}, u32[]{:S(2)}) collective-permute-start(f32[2,1024]{1,0:T(2,128)S(1)} %pad_maximum_fusion.15), channel_id=1, source_target_pairs={{0,2},{2,0},{4,6},{6,4},{8,10},{10,8},{12,14},{14,12},{16,18},{18,... | collective-permute-start | bytes 24584 | tf_op jit(solution)/shard_map/ppermute | solution.py:236
  985.3 3.7 collective-permute-start.17
  989.0 3.7 collective-permute-start.18
  992.7 5.5 collective-permute-start.19
  998.3 3.7 collective-permute-start.20
  (112 other events, 1708.7 us)
Sparse Core Ops, SparseCore 0:
  226.0 213.0 all-gather.5
